TPU v7x, 512 devices: a whole 4x4x16 slice. The times are simulated.
512 devices in a mesh: seq: 128 (over x, z, core), head: 4 (over y).
Axes of the slice: x: 4, y: 4, z: 16, core: 2. Of those that a mesh axis runs over, the one named last changes fastest.
Arguments:
- queries: bfloat16 [32768, 2048], P('seq', 'head'), may hold values from -10 to 10
- keys: bfloat16 [32768, 2048], P('seq', 'head'), may hold values from -10 to 10
- values: bfloat16 [32768, 2048], P('seq', 'head'), may hold values from -6 to 6
- out_grad: bfloat16 [32768, 2048], P('seq', 'head'), may hold values from -6 to 6
- cluster_ids: int32 [32768, 2], P('seq'), may hold values from 0 to 255, as said below
- slots: int32 [32768, 2], P('seq'), may hold values from 0 to 255, as said below
Outputs:
- attn_out: bfloat16 [32768, 2048], P('seq', 'head')
- grad_q: bfloat16 [32768, 2048], P('seq', 'head')
- grad_k: bfloat16 [32768, 2048], P('seq', 'head')
- grad_v: bfloat16 [32768, 2048], P('seq', 'head')
- cluster_means: float32 [256, 128], P('seq')
Inputs may be any that keep to these rules, and one draw needn't show every extreme that they name: `cluster_ids`: each cluster is named by exactly 256 of the 65536 ids, and a token's two ids differ. Clusters o * 2 to (o + 1) * 2 - 1 form group o. Of the 512 ids of each aligned block of 256 tokens, at most 8 name clusters of one group, and every block has a group that receives exactly 8 of them. The 256 members of each cluster hold the slots 0 to 255, each once, rising with the token index.
All inputs are finite; a program needn't handle non-finite values.
Results may differ from a plain program's by a relative error of at most 0.0094.
Values may be sent and summed in bfloat16 or wider, within the bound.
A program may use at most 64 MiB of HBM per device.

v0:
```python
import math

import jax
import jax.numpy as jnp
from jax import lax
from jax.sharding import PartitionSpec as P

HEAD_DIM = 128
CLUSTER_SIZE = 256


def attend(query_rows, key_rows, value_rows, score_scale):
    scores = (
        jnp.einsum("cqhd,ckhd->chqk", query_rows, key_rows, preferred_element_type=jnp.float32)
        * score_scale
    )
    slot_order = jnp.arange(query_rows.shape[1], dtype=jnp.int32)
    allowed = slot_order[None, :] <= slot_order[:, None]
    scores = jnp.where(allowed, scores, jnp.float32(-1e30))
    row_max = jnp.max(scores, axis=3, keepdims=True)
    weights = jnp.exp(scores - row_max)
    attention = weights / jnp.sum(weights, axis=3, keepdims=True)
    attn_low = attention.astype(jnp.bfloat16)
    attended = jnp.einsum(
        "chqk,ckhd->cqhd", attn_low, value_rows, preferred_element_type=jnp.float32
    )
    return (attention, attn_low, attended.astype(jnp.bfloat16))


def backprop(query_rows, key_rows, value_rows, grad_rows, attention, attn_low, score_scale):
    prob_grad = jnp.einsum(
        "cqhd,ckhd->chqk", grad_rows, value_rows, preferred_element_type=jnp.float32
    )
    row_dot = jnp.sum(attention * prob_grad, axis=3, keepdims=True)
    grad_score = (attention * (prob_grad - row_dot) * score_scale).astype(jnp.bfloat16)
    grad_query = jnp.einsum(
        "chqk,ckhd->cqhd", grad_score, key_rows, preferred_element_type=jnp.float32
    )
    grad_key = jnp.einsum(
        "chqk,cqhd->ckhd", grad_score, query_rows, preferred_element_type=jnp.float32
    )
    grad_value = jnp.einsum(
        "chqk,cqhd->ckhd", attn_low, grad_rows, preferred_element_type=jnp.float32
    )
    return (
        grad_query.astype(jnp.bfloat16),
        grad_key.astype(jnp.bfloat16),
        grad_value.astype(jnp.bfloat16),
    )


def key_centroids(key_rows):
    key_float = key_rows.astype(jnp.float32)
    normed = key_float * lax.rsqrt(jnp.mean(key_float * key_float, axis=3, keepdims=True) + 1e-06)
    return jnp.sum(normed, axis=(1, 2))


def local(queries, keys, values, out_grad, cluster_ids, slots):
    tok_rows = queries.shape[0]
    row_width = queries.shape[1]
    head_count = row_width // HEAD_DIM
    shards = lax.axis_size("seq")
    capacity = 4 * tok_rows // shards
    buffer_rows = shards * capacity
    clusters_here = 2 * tok_rows // CLUSTER_SIZE
    cluster_rows = clusters_here * CLUSTER_SIZE
    score_scale = 1.0 / math.sqrt(HEAD_DIM)
    owners = (cluster_ids // clusters_here).reshape(-1)
    owner_hits = (owners[:, None] == jnp.arange(shards, dtype=jnp.int32)[None, :]).astype(jnp.int32)
    earlier = jnp.cumsum(owner_hits, axis=0) - owner_hits
    buffer_slot = owners * capacity + jnp.sum(earlier * owner_hits, axis=1)
    targets = (cluster_ids % clusters_here * CLUSTER_SIZE + slots).reshape(-1)
    routing = jnp.full((buffer_rows,), -1, jnp.int32).at[buffer_slot].set(targets)
    slot_hits = buffer_slot[None, :] == jnp.arange(buffer_rows, dtype=jnp.int32)[:, None]
    dispatch = jnp.any(slot_hits.reshape(buffer_rows, tok_rows, 2), axis=2).astype(jnp.bfloat16)

    def pack_rows(rows_in):
        return jnp.dot(dispatch, rows_in, preferred_element_type=jnp.float32).astype(jnp.bfloat16)

    def unpack_rows(rows_in):
        summed = lax.dot_general(
            dispatch, rows_in, (((0,), (0,)), ((), ())), preferred_element_type=jnp.float32
        )
        return summed.astype(jnp.bfloat16)

    sent_query, sent_key, sent_value, sent_grad, routing_in = (
        lax.all_to_all(pack_rows(queries), "seq", split_axis=0, concat_axis=0, tiled=True),
        lax.all_to_all(pack_rows(keys), "seq", split_axis=0, concat_axis=0, tiled=True),
        lax.all_to_all(pack_rows(values), "seq", split_axis=0, concat_axis=0, tiled=True),
        lax.all_to_all(pack_rows(out_grad), "seq", split_axis=0, concat_axis=0, tiled=True),
        lax.all_to_all(routing, "seq", split_axis=0, concat_axis=0, tiled=True),
    )
    gather_table = (
        routing_in[None, :] == jnp.arange(cluster_rows, dtype=jnp.int32)[:, None]
    ).astype(jnp.bfloat16)

    def gather_rows(rows_in):
        grouped = jnp.dot(gather_table, rows_in, preferred_element_type=jnp.float32).astype(
            jnp.bfloat16
        )
        return grouped.reshape(clusters_here, CLUSTER_SIZE, head_count, HEAD_DIM)

    def scatter_rows(grouped):
        flat_rows = grouped.reshape(cluster_rows, row_width)
        spread = lax.dot_general(
            gather_table, flat_rows, (((0,), (0,)), ((), ())), preferred_element_type=jnp.float32
        )
        return spread.astype(jnp.bfloat16)

    query_rows = gather_rows(sent_query)
    key_rows = gather_rows(sent_key)
    value_rows = gather_rows(sent_value)
    attention, attn_low, attended = attend(query_rows, key_rows, value_rows, score_scale)
    totals = lax.psum(key_centroids(key_rows), "head")
    cluster_means = totals * lax.rsqrt(jnp.mean(totals * totals, axis=1, keepdims=True) + 1e-06)
    grad_rows = gather_rows(sent_grad)
    grad_query, grad_key, grad_value = backprop(
        query_rows, key_rows, value_rows, grad_rows, attention, attn_low, score_scale
    )
    back_out, back_query, back_key, back_value = (
        lax.all_to_all(scatter_rows(attended), "seq", split_axis=0, concat_axis=0, tiled=True),
        lax.all_to_all(scatter_rows(grad_query), "seq", split_axis=0, concat_axis=0, tiled=True),
        lax.all_to_all(scatter_rows(grad_key), "seq", split_axis=0, concat_axis=0, tiled=True),
        lax.all_to_all(scatter_rows(grad_value), "seq", split_axis=0, concat_axis=0, tiled=True),
    )
    return (
        unpack_rows(back_out),
        unpack_rows(back_query),
        unpack_rows(back_key),
        unpack_rows(back_value),
        cluster_means,
    )


def solution(mesh):
    placed = (
        P("seq", "head"),
        P("seq", "head"),
        P("seq", "head"),
        P("seq", "head"),
        P("seq", None),
        P("seq", None),
    )
    return jax.shard_map(
        local,
        mesh=mesh,
        in_specs=placed,
        out_specs=(
            P("seq", "head"),
            P("seq", "head"),
            P("seq", "head"),
            P("seq", "head"),
            P("seq", None),
        ),
        check_vma=False,
    )
```

profile of v0, /device:TPU:1, one launch (start us, length us, event | category | flops | bytes accessed | tf_op | source)
XLA Modules:
  0.0 546.8 jit_solution(7502052558362584254)
XLA Ops:
  4.6 2.4 scatter_custom_fusion
  7.8 20.4 %all-to-all-start = ((s32[128,8,1]{1,2,0:T(1,128)}), s32[128,8,1]{1,2,0:T(1,128)S(1)}, u32[]{:S(2)}, u32[]{:S(2)}) async-start(s32[128,8,1]{1,2,0:T(1,128)} %bitcast.5), calls=%async_computation | async-start | bytes 131072 | tf_op jit(solution)/shard_map/all_to_all | solution.py:91
  30.3 12.8 %all-to-all-done = s32[128,8,1]{1,2,0:T(1,128)S(1)} async-done(((s32[128,8,1]{1,2,0:T(1,128)}), s32[128,8,1]{1,2,0:T(1,128)S(1)}, u32[]{:S(2)}, u32[]{:S(2)}) %all-to-all-start) | async-done | bytes 4128 | tf_op jit(solution)/shard_map/all_to_all | solution.py:91
  43.1 6.6 %all-to-all-start.5 = ((bf16[128,8,512]{2,1,0:T(8,128)(2,1)}), bf16[128,8,512]{2,1,0:T(8,128)(2,1)S(1)}, u32[]{:S(2)}, u32[]{:S(2)}) async-start(bf16[128,8,512]{2,1,0:T(8,128)(2,1)} %fusion.28), calls=%async_computation.5 | async-start | bytes 2097152 | tf_op jit(solution)/shard_map/all_to_all | solution.py:90
  51.2 53.0 %all-to-all-done.5 = bf16[128,8,512]{2,1,0:T(8,128)(2,1)S(1)} async-done(((bf16[128,8,512]{2,1,0:T(8,128)(2,1)}), bf16[128,8,512]{2,1,0:T(8,128)(2,1)S(1)}, u32[]{:S(2)}, u32[]{:S(2)}) %all-to-all-start.5) | async-done | bytes 1048608 | tf_op jit(solution)/shard_map/all_to_all | solution.py:90
  104.2 8.5 %all-to-all-start.3 = ((bf16[128,8,512]{2,1,0:T(8,128)(2,1)}), bf16[128,8,512]{2,1,0:T(8,128)(2,1)S(1)}, u32[]{:S(2)}, u32[]{:S(2)}) async-start(bf16[128,8,512]{2,1,0:T(8,128)(2,1)} %fusion.27), calls=%async_computation.3 | async-start | bytes 2097152 | tf_op jit(solution)/shard_map/all_to_all | solution.py:88
  114.1 52.9 %all-to-all-done.3 = bf16[128,8,512]{2,1,0:T(8,128)(2,1)S(1)} async-done(((bf16[128,8,512]{2,1,0:T(8,128)(2,1)}), bf16[128,8,512]{2,1,0:T(8,128)(2,1)S(1)}, u32[]{:S(2)}, u32[]{:S(2)}) %all-to-all-start.3) | async-done | bytes 1048608 | tf_op jit(solution)/shard_map/all_to_all | solution.py:88
  167.0 9.0 %all-to-all-start.2 = ((bf16[128,8,512]{2,1,0:T(8,128)(2,1)}), bf16[128,8,512]{2,1,0:T(8,128)(2,1)}, u32[]{:S(2)}, u32[]{:S(2)}) async-start(bf16[128,8,512]{2,1,0:T(8,128)(2,1)} %fusion.26), calls=%async_computation.2 | async-start | bytes 2097152 | tf_op jit(solution)/shard_map/all_to_all | solution.py:87
  177.4 52.5 %all-to-all-done.2 = bf16[128,8,512]{2,1,0:T(8,128)(2,1)} async-done(((bf16[128,8,512]{2,1,0:T(8,128)(2,1)}), bf16[128,8,512]{2,1,0:T(8,128)(2,1)}, u32[]{:S(2)}, u32[]{:S(2)}) %all-to-all-start.2) | async-done | bytes 1048608 | tf_op jit(solution)/shard_map/all_to_all | solution.py:87
  230.0 8.5 %all-to-all-start.1 = ((bf16[128,8,512]{2,1,0:T(8,128)(2,1)}), bf16[128,8,512]{2,1,0:T(8,128)(2,1)S(1)}, u32[]{:S(2)}, u32[]{:S(2)}) async-start(bf16[128,8,512]{2,1,0:T(8,128)(2,1)} %fusion.25), calls=%async_computation.1 | async-start | bytes 2097152 | tf_op jit(solution)/shard_map/all_to_all | solution.py:89
  242.9 2.1 fusion.41
  246.2 2.8 fusion.40
  251.2 3.4 fusion.107
  254.7 2.1 fusion.44
  258.8 34.0 %all-to-all-done.1 = bf16[128,8,512]{2,1,0:T(8,128)(2,1)S(1)} async-done(((bf16[128,8,512]{2,1,0:T(8,128)(2,1)}), bf16[128,8,512]{2,1,0:T(8,128)(2,1)S(1)}, u32[]{:S(2)}, u32[]{:S(2)}) %all-to-all-start.1) | async-done | bytes 1048608 | tf_op jit(solution)/shard_map/all_to_all | solution.py:89
  292.8 8.5 %all-to-all-start.8 = ((bf16[128,8,512]{2,1,0:T(8,128)(2,1)}), bf16[128,8,512]{2,1,0:T(8,128)(2,1)S(1)}, u32[]{:S(2)}, u32[]{:S(2)}) async-start(bf16[128,8,512]{2,1,0:T(8,128)(2,1)} %fusion.29), calls=%async_computation.8 | async-start | bytes 2097152 | tf_op jit(solution)/shard_map/all_to_all | solution.py:124
  304.0 2.9 fusion.43
  310.0 45.7 %all-to-all-done.8 = bf16[128,8,512]{2,1,0:T(8,128)(2,1)S(1)} async-done(((bf16[128,8,512]{2,1,0:T(8,128)(2,1)}), bf16[128,8,512]{2,1,0:T(8,128)(2,1)S(1)}, u32[]{:S(2)}, u32[]{:S(2)}) %all-to-all-start.8) | async-done | bytes 1048608 | tf_op jit(solution)/shard_map/all_to_all | solution.py:124
  356.6 9.2 %all-to-all-start.4 = ((bf16[128,8,512]{2,1,0:T(8,128)(2,1)}), bf16[128,8,512]{2,1,0:T(8,128)(2,1)}, u32[]{:S(2)}, u32[]{:S(2)}) async-start(bf16[128,8,512]{2,1,0:T(8,128)(2,1)} %fusion.32), calls=%async_computation.4 | async-start | bytes 2097152 | tf_op jit(solution)/shard_map/all_to_all | solution.py:121
  367.4 4.0 fusion.48
  371.4 2.1 copy.155
  373.5 2.8 fusion.31
  376.3 43.5 %all-to-all-done.4 = bf16[128,8,512]{2,1,0:T(8,128)(2,1)} async-done(((bf16[128,8,512]{2,1,0:T(8,128)(2,1)}), bf16[128,8,512]{2,1,0:T(8,128)(2,1)}, u32[]{:S(2)}, u32[]{:S(2)}) %all-to-all-start.4) | async-done | bytes 1048608 | tf_op jit(solution)/shard_map/all_to_all | solution.py:121
  419.8 8.9 %all-to-all-start.6 = ((bf16[128,8,512]{2,1,0:T(8,128)(2,1)}), bf16[128,8,512]{2,1,0:T(8,128)(2,1)}, u32[]{:S(2)}, u32[]{:S(2)}) async-start(bf16[128,8,512]{2,1,0:T(8,128)(2,1)} %fusion.31), calls=%async_computation.6 | async-start | bytes 2097152 | tf_op jit(solution)/shard_map/all_to_all | solution.py:122
  428.7 4.0 fusion.45
  434.1 1.8 fusion.30
  435.8 46.9 %all-to-all-done.6 = bf16[128,8,512]{2,1,0:T(8,128)(2,1)} async-done(((bf16[128,8,512]{2,1,0:T(8,128)(2,1)}), bf16[128,8,512]{2,1,0:T(8,128)(2,1)}, u32[]{:S(2)}, u32[]{:S(2)}) %all-to-all-start.6) | async-done | bytes 1048608 | tf_op jit(solution)/shard_map/all_to_all | solution.py:122
  482.7 8.5 %all-to-all-start.7 = ((bf16[128,8,512]{2,1,0:T(8,128)(2,1)}), bf16[128,8,512]{2,1,0:T(8,128)(2,1)S(1)}, u32[]{:S(2)}, u32[]{:S(2)}) async-start(bf16[128,8,512]{2,1,0:T(8,128)(2,1)} %fusion.30), calls=%async_computation.7 | async-start | bytes 2097152 | tf_op jit(solution)/shard_map/all_to_all | solution.py:123
  492.6 9.3 %psum.7 = f32[2,128]{1,0:T(2,128)S(1)} all-reduce(f32[2,128]{1,0:T(2,128)S(1)} %fusion.52), channel_id=1, replica_groups=mesh['seq'=128,'head'=4] {'head'}, use_global_device_ids=true, to_apply=%region_10.11 | all-reduce | flops 256 | bytes 2048 | tf_op jit(solution)/shard_map/psum | solution.py:114
  503.9 2.4 convolution_convert_fusion.9
  506.3 2.4 convolution_convert_fusion.8
  508.7 36.9 %all-to-all-done.7 = bf16[128,8,512]{2,1,0:T(8,128)(2,1)S(1)} async-done(((bf16[128,8,512]{2,1,0:T(8,128)(2,1)}), bf16[128,8,512]{2,1,0:T(8,128)(2,1)S(1)}, u32[]{:S(2)}, u32[]{:S(2)}) %all-to-all-start.7) | async-done | bytes 1048608 | tf_op jit(solution)/shard_map/all_to_all | solution.py:123
  (73 shorter events, 35.1 us)
Async XLA Ops:
  0.6 28.2 %copy-start = (bf16[256,512]{1,0:T(8,128)(2,1)S(1)}, bf16[256,512]{1,0:T(8,128)(2,1)}, u32[]{:S(2)}) copy-start(bf16[256,512]{1,0:T(8,128)(2,1)} %param.9) | copy-start | bytes 786436
  7.8 35.4 %all-to-all-start = ((s32[128,8,1]{1,2,0:T(1,128)}), s32[128,8,1]{1,2,0:T(1,128)S(1)}, u32[]{:S(2)}, u32[]{:S(2)}) async-start(s32[128,8,1]{1,2,0:T(1,128)} %bitcast.5), calls=%async_computation | async-start | bytes 131072 | tf_op jit(solution)/shard_map/all_to_all | solution.py:91
  28.3 21.4 %copy-start.6 = (bf16[256,512]{1,0:T(8,128)(2,1)S(1)}, bf16[256,512]{1,0:T(8,128)(2,1)}, u32[]{:S(2)}) copy-start(bf16[256,512]{1,0:T(8,128)(2,1)} %param.7) | copy-start | bytes 786436
  43.1 61.0 %all-to-all-start.5 = ((bf16[128,8,512]{2,1,0:T(8,128)(2,1)}), bf16[128,8,512]{2,1,0:T(8,128)(2,1)S(1)}, u32[]{:S(2)}, u32[]{:S(2)}) async-start(bf16[128,8,512]{2,1,0:T(8,128)(2,1)} %fusion.28), calls=%async_computation.5 | async-start | bytes 2097152 | tf_op jit(solution)/shard_map/all_to_all | solution.py:90
  49.7 62.9 %copy-start.7 = (bf16[256,512]{1,0:T(8,128)(2,1)S(1)}, bf16[256,512]{1,0:T(8,128)(2,1)}, u32[]{:S(2)}) copy-start(bf16[256,512]{1,0:T(8,128)(2,1)} %param.6) | copy-start | bytes 786436
  104.2 62.8 %all-to-all-start.3 = ((bf16[128,8,512]{2,1,0:T(8,128)(2,1)}), bf16[128,8,512]{2,1,0:T(8,128)(2,1)S(1)}, u32[]{:S(2)}, u32[]{:S(2)}) async-start(bf16[128,8,512]{2,1,0:T(8,128)(2,1)} %fusion.27), calls=%async_computation.3 | async-start | bytes 2097152 | tf_op jit(solution)/shard_map/all_to_all | solution.py:88
  112.7 63.3 %copy-start.8 = (bf16[256,512]{1,0:T(8,128)(2,1)S(1)}, bf16[256,512]{1,0:T(8,128)(2,1)}, u32[]{:S(2)}) copy-start(bf16[256,512]{1,0:T(8,128)(2,1)} %param.8) | copy-start | bytes 786436
  167.0 63.0 %copy-start.5 = (bf16[128,8,512]{2,1,0:T(8,128)(2,1)}, bf16[128,8,512]{2,1,0:T(8,128)(2,1)S(1)}, u32[]{:S(2)}) copy-start(bf16[128,8,512]{2,1,0:T(8,128)(2,1)S(1)} %all-to-all-done.3) | copy-start | bytes 3145732
  167.0 62.9 %all-to-all-start.2 = ((bf16[128,8,512]{2,1,0:T(8,128)(2,1)}), bf16[128,8,512]{2,1,0:T(8,128)(2,1)}, u32[]{:S(2)}, u32[]{:S(2)}) async-start(bf16[128,8,512]{2,1,0:T(8,128)(2,1)} %fusion.26), calls=%async_computation.2 | async-start | bytes 2097152 | tf_op jit(solution)/shard_map/all_to_all | solution.py:87
  230.0 62.8 %all-to-all-start.1 = ((bf16[128,8,512]{2,1,0:T(8,128)(2,1)}), bf16[128,8,512]{2,1,0:T(8,128)(2,1)S(1)}, u32[]{:S(2)}, u32[]{:S(2)}) async-start(bf16[128,8,512]{2,1,0:T(8,128)(2,1)} %fusion.25), calls=%async_computation.1 | async-start | bytes 2097152 | tf_op jit(solution)/shard_map/all_to_all | solution.py:89
  242.9 11.8 %copy-start.1 = (bf16[2,256,4,128]{1,3,2,0:T(8,128)(2,1)}, bf16[2,256,4,128]{1,3,2,0:T(8,128)(2,1)S(1)}, u32[]{:S(2)}) copy-start(bf16[2,256,4,128]{1,3,2,0:T(8,128)(2,1)S(1)} %copy.159) | copy-start | bytes 1572868
  292.8 62.8 %all-to-all-start.8 = ((bf16[128,8,512]{2,1,0:T(8,128)(2,1)}), bf16[128,8,512]{2,1,0:T(8,128)(2,1)S(1)}, u32[]{:S(2)}, u32[]{:S(2)}) async-start(bf16[128,8,512]{2,1,0:T(8,128)(2,1)} %fusion.29), calls=%async_computation.8 | async-start | bytes 2097152 | tf_op jit(solution)/shard_map/all_to_all | solution.py:124
  304.0 3.0 copy-start.2
  355.7 1.0 copy-start.3
  356.6 63.2 %all-to-all-start.4 = ((bf16[128,8,512]{2,1,0:T(8,128)(2,1)}), bf16[128,8,512]{2,1,0:T(8,128)(2,1)}, u32[]{:S(2)}, u32[]{:S(2)}) async-start(bf16[128,8,512]{2,1,0:T(8,128)(2,1)} %fusion.32), calls=%async_computation.4 | async-start | bytes 2097152 | tf_op jit(solution)/shard_map/all_to_all | solution.py:121
  419.8 62.9 %all-to-all-start.6 = ((bf16[128,8,512]{2,1,0:T(8,128)(2,1)}), bf16[128,8,512]{2,1,0:T(8,128)(2,1)}, u32[]{:S(2)}, u32[]{:S(2)}) async-start(bf16[128,8,512]{2,1,0:T(8,128)(2,1)} %fusion.31), calls=%async_computation.6 | async-start | bytes 2097152 | tf_op jit(solution)/shard_map/all_to_all | solution.py:122
  435.8 66.9 %copy-start.4 = (bf16[128,8,512]{2,1,0:T(8,128)(2,1)S(1)}, bf16[128,8,512]{2,1,0:T(8,128)(2,1)}, u32[]{:S(2)}) copy-start(bf16[128,8,512]{2,1,0:T(8,128)(2,1)} %copy-done.3) | copy-start | bytes 3145732
  482.7 62.8 %all-to-all-start.7 = ((bf16[128,8,512]{2,1,0:T(8,128)(2,1)}), bf16[128,8,512]{2,1,0:T(8,128)(2,1)S(1)}, u32[]{:S(2)}, u32[]{:S(2)}) async-start(bf16[128,8,512]{2,1,0:T(8,128)(2,1)} %fusion.30), calls=%async_computation.7 | async-start | bytes 2097152 | tf_op jit(solution)/shard_map/all_to_all | solution.py:123
where the time goes:
time: 549 us; the launch traced here: 547 us
  waiting for transfers between devices  378 us (69%)
  starting transfers between devices  87.9 us (16%)
  matrix products  47 us (9%)
  local copies, waits for them, and re-layouts  18.6 us (3%)
  blocking collectives  9.32 us (2%)
    all_to_all x1, waiting for transfers between devices, local(): lax.all_to_all(pack_rows(out_grad), 'seq', split_axis=0, concat_axis=0, t...  53 us
    all_to_all x1, waiting for transfers between devices, local(): lax.all_to_all(pack_rows(keys), 'seq', split_axis=0, concat_axis=0, tiled...  52.9 us
    all_to_all x1, waiting for transfers between devices, local(): lax.all_to_all(pack_rows(queries), 'seq', split_axis=0, concat_axis=0, ti...  52.5 us
    all_to_all x1, waiting for transfers between devices, local(): lax.all_to_all(scatter_rows(grad_query), 'seq', split_axis=0, concat_axis...  46.9 us
    all_to_all x1, waiting for transfers between devices, local(): lax.all_to_all(scatter_rows(grad_value), 'seq', split_axis=0, concat_axis...  45.7 us
    all_to_all x1, waiting for transfers between devices, local(): lax.all_to_all(scatter_rows(attended), 'seq', split_axis=0, concat_axis=0...  43.5 us
    all_to_all x1, waiting for transfers between devices, local(): lax.all_to_all(scatter_rows(grad_key), 'seq', split_axis=0, concat_axis=0...  36.9 us
    all_to_all x1, waiting for transfers between devices, local(): lax.all_to_all(pack_rows(values), 'seq', split_axis=0, concat_axis=0, til...  34 us
  transfers between devices with their start and end apart: 9, of which 9 were waited for; matrix products, arithmetic and copies ran while one was open for 11% of the time, Pallas kernels for 0%

commit v1 on v0

--- a/solution.py
+++ b/solution.py
@@ -1,8 +1,11 @@
+import functools
 import math
 
 import jax
 import jax.numpy as jnp
 from jax import lax
+from jax.experimental import pallas as pl
+from jax.experimental.pallas import tpu as pltpu
 from jax.sharding import PartitionSpec as P
 
 HEAD_DIM = 128
@@ -53,6 +56,67 @@
     key_float = key_rows.astype(jnp.float32)
     normed = key_float * lax.rsqrt(jnp.mean(key_float * key_float, axis=3, keepdims=True) + 1e-06)
     return jnp.sum(normed, axis=(1, 2))
+
+
+def exchange_kernel(shards, send_ref, out_ref, send_sem, recv_sem, own_sem):
+    me = lax.axis_index("seq")
+    head = lax.axis_index("head")
+    barrier = pltpu.get_barrier_semaphore()
+
+    def greet(step, carry):
+        peer = lax.rem(me + step, shards)
+        pl.semaphore_signal(
+            barrier, inc=1, device_id=(peer, head), device_id_type=pl.DeviceIdType.MESH
+        )
+        return carry
+
+    lax.fori_loop(1, shards, greet, 0)
+    own = pltpu.make_async_copy(send_ref.at[me], out_ref.at[me], own_sem)
+    own.start()
+    pl.semaphore_wait(barrier, shards - 1)
+
+    def send(step, carry):
+        peer = lax.rem(me + step, shards)
+        pltpu.make_async_remote_copy(
+            src_ref=send_ref.at[peer],
+            dst_ref=out_ref.at[me],
+            send_sem=send_sem,
+            recv_sem=recv_sem,
+            device_id=(peer, head),
+            device_id_type=pl.DeviceIdType.MESH,
+        ).start()
+        return carry
+
+    lax.fori_loop(1, shards, send, 0)
+    own.wait()
+    whole = pltpu.make_async_remote_copy(
+        src_ref=send_ref.at[pl.ds(0, shards - 1)],
+        dst_ref=out_ref.at[pl.ds(0, shards - 1)],
+        send_sem=send_sem,
+        recv_sem=recv_sem,
+        device_id=(lax.rem(me + 1, shards), head),
+        device_id_type=pl.DeviceIdType.MESH,
+    )
+    whole.wait_send()
+    whole.wait_recv()
+
+
+def exchange(boxes, collective_id):
+    shards = boxes.shape[0]
+    return pl.pallas_call(
+        functools.partial(exchange_kernel, shards),
+        out_shape=jax.ShapeDtypeStruct(boxes.shape, boxes.dtype),
+        in_specs=[pl.BlockSpec(memory_space=pltpu.VMEM)],
+        out_specs=pl.BlockSpec(memory_space=pltpu.VMEM),
+        scratch_shapes=[
+            pltpu.SemaphoreType.DMA,
+            pltpu.SemaphoreType.DMA,
+            pltpu.SemaphoreType.DMA,
+        ],
+        compiler_params=pltpu.CompilerParams(
+            collective_id=collective_id, has_side_effects=True, vmem_limit_bytes=24 * 2**20
+        ),
+    )(boxes)
 
 
 def local(queries, keys, values, out_grad, cluster_ids, slots):
@@ -83,13 +147,19 @@
         )
         return summed.astype(jnp.bfloat16)
 
-    sent_query, sent_key, sent_value, sent_grad, routing_in = (
-        lax.all_to_all(pack_rows(queries), "seq", split_axis=0, concat_axis=0, tiled=True),
-        lax.all_to_all(pack_rows(keys), "seq", split_axis=0, concat_axis=0, tiled=True),
-        lax.all_to_all(pack_rows(values), "seq", split_axis=0, concat_axis=0, tiled=True),
-        lax.all_to_all(pack_rows(out_grad), "seq", split_axis=0, concat_axis=0, tiled=True),
-        lax.all_to_all(routing, "seq", split_axis=0, concat_axis=0, tiled=True),
-    )
+    routing_in = lax.all_to_all(routing, "seq", split_axis=0, concat_axis=0, tiled=True)
+
+    def box(rows_in):
+        return rows_in.reshape(shards, capacity, row_width)
+
+    def unbox(boxes, index):
+        part = boxes[:, index * capacity : (index + 1) * capacity]
+        return part.reshape(buffer_rows, row_width)
+
+    arrived = exchange(
+        jnp.concatenate([box(pack_rows(a)) for a in (queries, keys, values, out_grad)], axis=1), 0
+    )
+    sent_query, sent_key, sent_value, sent_grad = (unbox(arrived, i) for i in range(4))
     gather_table = (
         routing_in[None, :] == jnp.arange(cluster_rows, dtype=jnp.int32)[:, None]
     ).astype(jnp.bfloat16)
@@ -117,12 +187,13 @@
     grad_query, grad_key, grad_value = backprop(
         query_rows, key_rows, value_rows, grad_rows, attention, attn_low, score_scale
     )
-    back_out, back_query, back_key, back_value = (
-        lax.all_to_all(scatter_rows(attended), "seq", split_axis=0, concat_axis=0, tiled=True),
-        lax.all_to_all(scatter_rows(grad_query), "seq", split_axis=0, concat_axis=0, tiled=True),
-        lax.all_to_all(scatter_rows(grad_key), "seq", split_axis=0, concat_axis=0, tiled=True),
-        lax.all_to_all(scatter_rows(grad_value), "seq", split_axis=0, concat_axis=0, tiled=True),
-    )
+    returned = exchange(
+        jnp.concatenate(
+            [box(scatter_rows(a)) for a in (attended, grad_query, grad_key, grad_value)], axis=1
+        ),
+        1,
+    )
+    back_out, back_query, back_key, back_value = (unbox(returned, i) for i in range(4))
     return (
         unpack_rows(back_out),
         unpack_rows(back_query),

time: 549 us -> 486 us (0.89)
  Pallas kernels: 0 us -> 392 us
  waiting for transfers between devices: 378 us -> 0.01 us
  starting transfers between devices: 87.9 us -> 20.5 us
  matrix products: 47 us -> 37.3 us
    pallas_call x0 -> x2, Pallas kernels: none -> 392 us  [exchange(): pl.pallas_call(functools.partial(exchange_kernel, shards), out_shape=jax....]
    all_to_all x8 -> x0, waiting for transfers between devices: 365 us -> none  [the longest x1 53 us: local(): lax.all_to_all(pack_rows(out_grad), 'seq', split_axis=0, concat_axis=0, t...]
    all_to_all x8 -> x0, starting transfers between devices: 67.5 us -> none  [the longest x1 9.16 us: local(): lax.all_to_all(scatter_rows(attended), 'seq', split_axis=0, concat_axis=0...]
    all_to_all x1, waiting for transfers between devices: 12.8 us -> 0.01 us  [local(): lax.all_to_all(routing, 'seq', split_axis=0, concat_axis=0, tiled=True)]
  transfers between devices with their start and end apart: 9 -> 1, of which waited for: 9 -> 0; matrix products, arithmetic and copies ran while one was open for 11% -> 1% of each run, Pallas kernels for 0% -> 41%
where the time goes in v1:
time: 486 us; the launch traced here: 484 us
  Pallas kernels  392 us (81%)
  matrix products  37.3 us (8%)
  starting transfers between devices  20.5 us (4%)
  local copies, waits for them, and re-layouts  18.5 us (4%)
  blocking collectives  8.74 us (2%)
  other arithmetic  6.02 us (1%)
    pallas_call x2, Pallas kernels, exchange(): pl.pallas_call(functools.partial(exchange_kernel, shards), out_shape=jax....  392 us
    all_to_all x1, starting transfers between devices, local(): lax.all_to_all(routing, 'seq', split_axis=0, concat_axis=0, tiled=True)  20.5 us
  transfers between devices with their start and end apart: 1, of which 0 were waited for; matrix products, arithmetic and copies ran while one was open for 1% of the time, Pallas kernels for 41%

profile of v1, /device:TPU:1, one launch (start us, length us, event | category | flops | bytes accessed | tf_op | source)
XLA Modules:
  0.0 484.1 jit_solution(12915311223934396728)
XLA Ops:
  1.4 0.8 copy.134
  2.4 0.8 copy.144
  4.6 2.4 scatter_custom_fusion
  7.8 20.5 %all-to-all-start = ((s32[128,8,1]{1,2,0:T(1,128)}), s32[128,8,1]{1,2,0:T(1,128)S(1)}, u32[]{:S(2)}, u32[]{:S(2)}) async-start(s32[128,8,1]{1,2,0:T(1,128)} %bitcast.5), calls=%async_computation | async-start | bytes 131072 | tf_op jit(solution)/shard_map/all_to_all | solution.py:150
  31.5 196.2 %shard_map.101 = bf16[128,32,512]{2,1,0:T(8,128)(2,1)S(1)} custom-call(bf16[128,32,512]{2,1,0:T(8,128)(2,1)S(1)} %pad_maximum_fusion.send_ref), custom_call_target="tpu_custom_call" | custom-call | tf_op jit(solution)/shard_map/pallas_call | solution.py:106
  227.7 1.9 copy-done.1
  230.1 0.8 reduce.3
  231.0 1.9 fusion.42
  233.0 1.9 fusion.41
  236.0 2.9 fusion.40
  238.9 1.9 fusion.39
  241.4 1.4 reshape.180
  242.8 1.1 copy.156
  243.9 3.3 fusion.115
  247.2 3.0 fusion.44
  250.2 1.2 fusion.43
  251.4 1.5 fusion.93
  252.9 4.0 fusion.48
  256.8 4.0 fusion.45
  260.8 1.4 copy.161
  262.2 0.8 fusion.29
  263.0 1.1 copy.150
  264.0 1.8 fusion.32
  265.8 2.1 copy.158
  267.9 2.1 copy.155
  270.0 1.9 fusion.31
  273.3 195.8 %shard_map.102 = bf16[128,32,512]{2,1,0:T(8,128)(2,1)S(1)} custom-call(bf16[128,32,512]{2,1,0:T(8,128)(2,1)S(1)} %pad_maximum_fusion.1.send_ref), custom_call_target="tpu_custom_call" | custom-call | tf_op jit(solution)/shard_map/pallas_call | solution.py:106
  469.1 1.2 convolution_convert_fusion.6
  470.3 1.2 convolution_convert_fusion.7
  471.5 1.2 convolution_convert_fusion.8
  472.7 1.2 convolution_convert_fusion.9
  474.6 8.7 %psum.7 = f32[2,128]{1,0:T(2,128)S(1)} all-reduce(f32[2,128]{1,0:T(2,128)S(1)} %fusion.52), channel_id=1, replica_groups=mesh['seq'=128,'head'=4] {'head'}, use_global_device_ids=true, to_apply=%region_10.11 | all-reduce | flops 256 | bytes 2048 | tf_op jit(solution)/shard_map/psum | solution.py:184
  (67 shorter events, 11.2 us)
Async XLA Ops:
  0.6 28.3 %copy-start = (bf16[256,512]{1,0:T(8,128)(2,1)S(1)}, bf16[256,512]{1,0:T(8,128)(2,1)}, u32[]{:S(2)}) copy-start(bf16[256,512]{1,0:T(8,128)(2,1)} %param.9) | copy-start | bytes 786436
  4.2 25.2 %copy-start.8 = (bf16[256,512]{1,0:T(8,128)(2,1)S(1)}, bf16[256,512]{1,0:T(8,128)(2,1)}, u32[]{:S(2)}) copy-start(bf16[256,512]{1,0:T(8,128)(2,1)} %param.8) | copy-start | bytes 786436
  7.8 22.1 %copy-start.9 = (bf16[256,512]{1,0:T(8,128)(2,1)S(1)}, bf16[256,512]{1,0:T(8,128)(2,1)}, u32[]{:S(2)}) copy-start(bf16[256,512]{1,0:T(8,128)(2,1)} %param.7) | copy-start | bytes 786436
  7.8 221.9 %all-to-all-start = ((s32[128,8,1]{1,2,0:T(1,128)}), s32[128,8,1]{1,2,0:T(1,128)S(1)}, u32[]{:S(2)}, u32[]{:S(2)}) async-start(s32[128,8,1]{1,2,0:T(1,128)} %bitcast.5), calls=%async_computation | async-start | bytes 131072 | tf_op jit(solution)/shard_map/all_to_all | solution.py:150
  29.0 1.4 copy-start.10
  227.7 1.9 copy-start.1
  236.0 8.0 %copy-start.5 = (bf16[2,256,4,128]{1,3,2,0:T(8,128)(2,1)}, bf16[2,256,4,128]{1,3,2,0:T(8,128)(2,1)S(1)}, u32[]{:S(2)}) copy-start(bf16[2,256,4,128]{1,3,2,0:T(8,128)(2,1)S(1)} %copy.153) | copy-start | bytes 1572868
  241.3 5.9 %copy-start.2 = (bf16[2,256,4,128]{1,3,2,0:T(8,128)(2,1)}, bf16[2,256,4,128]{1,3,2,0:T(8,128)(2,1)S(1)}, u32[]{:S(2)}) copy-start(bf16[2,256,4,128]{1,3,2,0:T(8,128)(2,1)S(1)} %copy.159) | copy-start | bytes 1572868
  241.4 8.8 %copy-start.4 = (bf16[2,256,4,128]{3,2,1,0:T(4,128)(2,1)}, bf16[2,256,4,128]{3,2,1,0:T(4,128)(2,1)S(1)}, u32[]{:S(2)}) copy-start(bf16[2,256,4,128]{3,2,1,0:T(4,128)(2,1)S(1)} %reshape.178) | copy-start | bytes 1572868
  247.2 3.0 copy-start.11
  250.2 1.2 copy-start.3
  260.8 2.1 copy-start.6
  270.0 1.9 copy-start.7

commit v2 on v0

--- a/solution.py
+++ b/solution.py
@@ -1,12 +1,441 @@
+import functools
 import math
 
 import jax
 import jax.numpy as jnp
 from jax import lax
+from jax.experimental import pallas as pl
+from jax.experimental.pallas import tpu as pltpu
 from jax.sharding import PartitionSpec as P
 
 HEAD_DIM = 128
 CLUSTER_SIZE = 256
+RING = 16
+PLANE = 8
+REACH = 4
+MESH = pl.DeviceIdType.MESH
+
+
+def far_planes(way, pair):
+    return 4 if way == pair else 3
+
+
+def place():
+    me = lax.axis_index("seq")
+    head = lax.axis_index("head")
+    return (me, head, me // (2 * RING), lax.rem(me // 2, RING), lax.rem(me, 2))
+
+
+def device_at(column, height, core):
+    return (column * RING + lax.rem(height + RING, RING)) * 2 + core
+
+
+def greet_all(me, head, shards):
+    barrier = pltpu.get_barrier_semaphore()
+
+    def greet(step, carry):
+        peer = lax.rem(me + step, shards)
+        pl.semaphore_signal(barrier, inc=1, device_id=(peer, head), device_id_type=MESH)
+        return carry
+
+    lax.fori_loop(1, shards, greet, 0)
+    return barrier
+
+
+def hit_table(slot_rows, height):
+    rows, lanes = (2 * PLANE * 8, slot_rows.shape[1])
+    row = lax.broadcasted_iota(jnp.int32, (rows, lanes), 0)
+    lane = lax.broadcasted_iota(jnp.int32, (rows, lanes), 1)
+    group = device_at(row // 32, height, row // 16 % 2)
+    wanted = group * 8 + row % 8
+    hit = (slot_rows[0:1, :] == wanted) | (slot_rows[1:2, :] == wanted)
+    same = row // 8 % 2 == lane // (lanes // 2)
+    return jnp.where(hit & same, 1.0, 0.0).astype(jnp.bfloat16)
+
+
+def spread_kernel(
+    shards, rows_ref, slots_ref, targets_ref, boxes_ref, held_slots_ref, held_targets_ref,
+    passing, near_box, far_box, slot_send, slot_recv, target_send, target_recv,
+    pass_send, pass_recv, box_send, box_recv, own_sem,
+):
+    me, head, column, height, core = place()
+    mine = column * 2 + core
+    barrier = greet_all(me, head, shards)
+    held_slots_ref[2 * REACH] = slots_ref[...]
+    held_targets_ref[me] = targets_ref[me]
+    pl.semaphore_wait(barrier, shards - 1)
+
+    def slot_copy(way, hop):
+        step = hop if way == 0 else -hop
+        return pltpu.make_async_remote_copy(
+            src_ref=slots_ref,
+            dst_ref=held_slots_ref.at[way * REACH + hop - 1],
+            send_sem=slot_send,
+            recv_sem=slot_recv,
+            device_id=(device_at(column, height + step, core), head),
+            device_id_type=MESH,
+        )
+
+    def pass_on(way, hop, pair):
+        step = 1 if way == 0 else -1
+        source = rows_ref.at[pair] if hop == 0 else passing.at[way, hop - 1, pair]
+        return pltpu.make_async_remote_copy(
+            src_ref=source,
+            dst_ref=passing.at[way, hop, pair],
+            send_sem=pass_send.at[way, hop, pair],
+            recv_sem=pass_recv.at[way, hop, pair],
+            device_id=(device_at(column, height + step, core), head),
+            device_id_type=MESH,
+        )
+
+    def box_copy(source, block, pair, place_to):
+        return pltpu.make_async_remote_copy(
+            src_ref=source,
+            dst_ref=boxes_ref.at[block, pair],
+            send_sem=box_send,
+            recv_sem=box_recv,
+            device_id=(place_to, head),
+            device_id_type=MESH,
+        )
+
+    for way in range(2):
+        for hop in range(1, REACH + 1):
+            slot_copy(way, hop).start()
+    for pair in range(2):
+        for way in range(2):
+            pass_on(way, 0, pair).start()
+
+    def send_target(step, carry):
+        peer = lax.rem(me + step, shards)
+        pltpu.make_async_remote_copy(
+            src_ref=targets_ref.at[peer],
+            dst_ref=held_targets_ref.at[me],
+            send_sem=target_send,
+            recv_sem=target_recv,
+            device_id=(peer, head),
+            device_id_type=MESH,
+        ).start()
+        return carry
+
+    lax.fori_loop(1, shards, send_target, 0)
+
+    def deliver_near(block_rows, slot_rows, block_height, index, pair):
+        table = hit_table(slot_rows, height)
+        packed = jnp.dot(table, block_rows, preferred_element_type=jnp.float32)
+        near_box[index, pair] = packed.astype(jnp.bfloat16).reshape(PLANE, 16, -1)
+        block = device_at(column, block_height, core)
+        pltpu.make_async_copy(
+            near_box.at[index, pair, mine], boxes_ref.at[block, pair], own_sem
+        ).start()
+
+        def send(step, carry):
+            peer = lax.rem(mine + step, PLANE)
+            box_copy(
+                near_box.at[index, pair, peer], block, pair,
+                device_at(peer // 2, height, lax.rem(peer, 2)),
+            ).start()
+            return carry
+
+        lax.fori_loop(1, PLANE, send, 0)
+
+    def deliver_far(block_rows, slot_rows, way, pair):
+        sign = 1 if way == 0 else -1
+        block = device_at(column, height - sign * REACH, core)
+        for away in range(far_planes(way, pair), 0, -1):
+            there = height + sign * away
+            table = hit_table(slot_rows, there)
+            packed = jnp.dot(table, block_rows, preferred_element_type=jnp.float32)
+            far_box[way, pair, away - 1] = packed.astype(jnp.bfloat16).reshape(PLANE, 16, -1)
+
+            def send(step, carry):
+                peer = lax.rem(mine + step, PLANE)
+                box_copy(
+                    far_box.at[way, pair, away - 1, peer], block, pair,
+                    device_at(peer // 2, there, lax.rem(peer, 2)),
+                ).start()
+                return carry
+
+            lax.fori_loop(0, PLANE, send, 0)
+
+    for pair in range(2):
+        deliver_near(rows_ref[pair], slots_ref[...], height, 2 * REACH, pair)
+    every = pltpu.make_async_remote_copy(
+        src_ref=held_slots_ref.at[pl.ds(0, 2 * REACH)],
+        dst_ref=held_slots_ref.at[pl.ds(0, 2 * REACH)],
+        send_sem=slot_send,
+        recv_sem=slot_recv,
+        device_id=(device_at(column, height + 1, core), head),
+        device_id_type=MESH,
+    )
+    every.wait_send()
+    every.wait_recv()
+    for hop in range(1, REACH + 1):
+        for pair in range(2):
+            for way in range(2):
+                pass_on(way, hop - 1, pair).wait_recv()
+                if hop < REACH:
+                    pass_on(way, hop, pair).start()
+                index = way * REACH + hop - 1
+                block_rows = passing[way, hop - 1, pair]
+                if hop == REACH:
+                    deliver_far(block_rows, held_slots_ref[index], way, pair)
+                block_height = height - hop if way == 0 else height + hop
+                deliver_near(block_rows, held_slots_ref[index], block_height, index, pair)
+    for hop in range(REACH):
+        for pair in range(2):
+            for way in range(2):
+                pass_on(way, hop, pair).wait_send()
+    for index in range(2 * REACH + 1):
+        for pair in range(2):
+            pltpu.make_async_copy(
+                near_box.at[index, pair, mine], boxes_ref.at[0, pair], own_sem
+            ).wait()
+    remote = shards - (2 * REACH + 1)
+    lot = pltpu.make_async_remote_copy(
+        src_ref=boxes_ref.at[pl.ds(0, remote)],
+        dst_ref=boxes_ref.at[pl.ds(0, remote)],
+        send_sem=box_send,
+        recv_sem=box_recv,
+        device_id=(device_at(column, height + 1, core), head),
+        device_id_type=MESH,
+    )
+    lot.wait_send()
+    lot.wait_recv()
+    lines = pltpu.make_async_remote_copy(
+        src_ref=targets_ref.at[pl.ds(0, shards - 1)],
+        dst_ref=held_targets_ref.at[pl.ds(0, shards - 1)],
+        send_sem=target_send,
+        recv_sem=target_recv,
+        device_id=(device_at(column, height + 1, core), head),
+        device_id_type=MESH,
+    )
+    lines.wait_send()
+    lines.wait_recv()
+
+
+def spread(rows, slots, targets):
+    shards = targets.shape[0]
+    _, count, width = rows.shape
+    vmem = pl.BlockSpec(memory_space=pltpu.VMEM)
+    dma = pltpu.SemaphoreType.DMA
+    return pl.pallas_call(
+        functools.partial(spread_kernel, shards),
+        out_shape=(
+            jax.ShapeDtypeStruct((shards, 2, 16, width), jnp.bfloat16),
+            jax.ShapeDtypeStruct((2 * REACH + 1,) + slots.shape, jnp.int32),
+            jax.ShapeDtypeStruct(targets.shape, jnp.int32),
+        ),
+        in_specs=[vmem] * 3,
+        out_specs=(vmem,) * 3,
+        scratch_shapes=[
+            pltpu.VMEM((2, REACH, 2, count, width), jnp.bfloat16),
+            pltpu.VMEM((2 * REACH + 1, 2, PLANE, 16, width), jnp.bfloat16),
+            pltpu.VMEM((2, 2, 4, PLANE, 16, width), jnp.bfloat16),
+            dma, dma, dma, dma,
+            dma((2, REACH, 2)), dma((2, REACH, 2)),
+            dma, dma, dma,
+        ],
+        compiler_params=pltpu.CompilerParams(
+            collective_id=0, has_side_effects=True, vmem_limit_bytes=48 * 2**20
+        ),
+    )(rows, slots, targets)
+
+
+def collect_kernel(
+    shards, boxes_ref, held_slots_ref, sums_ref, rows_ref, totals_ref,
+    passing, near_box, far_box, sums, pass_send, pass_recv, near_send, near_recv, own_sem,
+    far_send, far_recv, sum_send, sum_recv,
+):
+    me, head, column, height, core = place()
+    mine = column * 2 + core
+    heads = sums.shape[0]
+    barrier = greet_all(me, head, shards)
+
+    def other_head(step):
+        return (me, lax.rem(head + step, heads))
+
+    for step in range(1, heads):
+        pl.semaphore_signal(barrier, inc=1, device_id=other_head(step), device_id_type=MESH)
+    sums[head] = sums_ref[...]
+    pl.semaphore_wait(barrier, shards - 1 + heads - 1)
+
+    def pass_on(way, hop, pair):
+        step = -1 if way == 0 else 1
+        return pltpu.make_async_remote_copy(
+            src_ref=passing.at[way, hop, pair],
+            dst_ref=passing.at[way, hop - 1, pair],
+            send_sem=pass_send.at[way, hop - 1, pair],
+            recv_sem=pass_recv.at[way, hop - 1, pair],
+            device_id=(device_at(column, height + step, core), head),
+            device_id_type=MESH,
+        )
+
+    for pair in range(2):
+        for way in range(2):
+            sign = 1 if way == 0 else -1
+            for away in range(far_planes(way, pair), 0, -1):
+
+                def send_far(step, carry):
+                    peer = lax.rem(mine + step, PLANE)
+                    block = device_at(
+                        peer // 2, height - sign * (REACH + away), lax.rem(peer, 2)
+                    )
+                    relay = device_at(peer // 2, height - sign * away, lax.rem(peer, 2))
+                    pltpu.make_async_remote_copy(
+                        src_ref=boxes_ref.at[block, pair],
+                        dst_ref=far_box.at[way, pair, away - 1, mine],
+                        send_sem=far_send.at[way, pair],
+                        recv_sem=far_recv.at[way, pair],
+                        device_id=(relay, head),
+                        device_id_type=MESH,
+                    ).start()
+                    return carry
+
+                lax.fori_loop(0, PLANE, send_far, 0)
+    for step in range(1, heads):
+        pltpu.make_async_remote_copy(
+            src_ref=sums_ref,
+            dst_ref=sums.at[head],
+            send_sem=sum_send,
+            recv_sem=sum_recv,
+            device_id=other_head(step),
+            device_id_type=MESH,
+        ).start()
+
+    def near_height(index):
+        if index == 2 * REACH:
+            return height
+        hop = index % REACH + 1
+        return height - hop if index < REACH else height + hop
+
+    order = [way * REACH + hop - 1 for hop in range(REACH, 0, -1) for way in range(2)]
+    for index in order + [2 * REACH]:
+        for pair in range(2):
+            own = device_at(column, near_height(index), core)
+            pltpu.make_async_copy(
+                boxes_ref.at[own, pair], near_box.at[index, pair, mine], own_sem.at[index, pair]
+            ).start()
+
+            def send_near(step, carry):
+                peer = lax.rem(mine + step, PLANE)
+                block = device_at(peer // 2, near_height(index), lax.rem(peer, 2))
+                pltpu.make_async_remote_copy(
+                    src_ref=boxes_ref.at[block, pair],
+                    dst_ref=near_box.at[index, pair, mine],
+                    send_sem=near_send.at[index, pair],
+                    recv_sem=near_recv.at[index, pair],
+                    device_id=(device_at(peer // 2, height, lax.rem(peer, 2)), head),
+                    device_id_type=MESH,
+                ).start()
+                return carry
+
+            lax.fori_loop(1, PLANE, send_near, 0)
+
+    def await_near(index, pair):
+        pltpu.make_async_copy(
+            boxes_ref.at[0, pair], near_box.at[index, pair, 0], own_sem.at[index, pair]
+        ).wait()
+        lot = near_box.at[index, pair, pl.ds(0, PLANE - 1)]
+        copy = pltpu.make_async_remote_copy(
+            src_ref=lot,
+            dst_ref=lot,
+            send_sem=near_send.at[index, pair],
+            recv_sem=near_recv.at[index, pair],
+            device_id=other_head(1),
+            device_id_type=MESH,
+        )
+        copy.wait_send()
+        copy.wait_recv()
+
+    def unpack(slot_rows, there, packed):
+        table = hit_table(slot_rows, there)
+        return lax.dot_general(
+            table, packed.reshape(2 * PLANE * 8, -1), (((0,), (0,)), ((), ())),
+            preferred_element_type=jnp.float32,
+        )
+
+    for hop in range(REACH, 0, -1):
+        for pair in range(2):
+            for way in range(2):
+                index = way * REACH + hop - 1
+                slot_rows = held_slots_ref[index]
+                await_near(index, pair)
+                total = unpack(slot_rows, height, near_box[index, pair])
+                if hop == REACH:
+                    planes = far_planes(way, pair)
+                    lot = far_box.at[way, pair, pl.ds(0, planes)]
+                    copy = pltpu.make_async_remote_copy(
+                        src_ref=lot,
+                        dst_ref=lot,
+                        send_sem=far_send.at[way, pair],
+                        recv_sem=far_recv.at[way, pair],
+                        device_id=other_head(1),
+                        device_id_type=MESH,
+                    )
+                    copy.wait_send()
+                    copy.wait_recv()
+                    for away in range(1, planes + 1):
+                        there = height + away if way == 0 else height - away
+                        total += unpack(slot_rows, there, far_box[way, pair, away - 1])
+                else:
+                    pass_on(way, hop + 1, pair).wait_recv()
+                    total += passing[way, hop, pair].astype(jnp.float32)
+                passing[way, hop, pair] = total.astype(jnp.bfloat16)
+                pass_on(way, hop, pair).start()
+    for pair in range(2):
+        await_near(2 * REACH, pair)
+        total = unpack(held_slots_ref[2 * REACH], height, near_box[2 * REACH, pair])
+        for way in range(2):
+            pass_on(way, 1, pair).wait_recv()
+            total += passing[way, 0, pair].astype(jnp.float32)
+        rows_ref[pair] = total.astype(jnp.bfloat16)
+    for hop in range(REACH, 0, -1):
+        for pair in range(2):
+            for way in range(2):
+                pass_on(way, hop, pair).wait_send()
+    lines = pltpu.make_async_remote_copy(
+        src_ref=sums.at[pl.ds(0, heads - 1)],
+        dst_ref=sums.at[pl.ds(0, heads - 1)],
+        send_sem=sum_send,
+        recv_sem=sum_recv,
+        device_id=other_head(1),
+        device_id_type=MESH,
+    )
+    lines.wait_send()
+    lines.wait_recv()
+    grand = sums[0]
+    for step in range(1, heads):
+        grand += sums[step]
+    totals_ref[...] = grand * lax.rsqrt(jnp.mean(grand * grand, axis=1, keepdims=True) + 1e-06)
+
+
+def collect(boxes, held_slots, sums):
+    shards, _, _, width = boxes.shape
+    count = held_slots.shape[2]
+    heads = lax.axis_size("head")
+    vmem = pl.BlockSpec(memory_space=pltpu.VMEM)
+    dma = pltpu.SemaphoreType.DMA
+    return pl.pallas_call(
+        functools.partial(collect_kernel, shards),
+        out_shape=(
+            jax.ShapeDtypeStruct((2, count, width), jnp.bfloat16),
+            jax.ShapeDtypeStruct(sums.shape, jnp.float32),
+        ),
+        in_specs=[vmem] * 3,
+        out_specs=(vmem,) * 2,
+        scratch_shapes=[
+            pltpu.VMEM((2, REACH + 1, 2, count, width), jnp.bfloat16),
+            pltpu.VMEM((2 * REACH + 1, 2, PLANE, 16, width), jnp.bfloat16),
+            pltpu.VMEM((2, 2, 4, PLANE, 16, width), jnp.bfloat16),
+            pltpu.VMEM((heads,) + sums.shape, jnp.float32),
+            dma((2, REACH, 2)), dma((2, REACH, 2)),
+            dma((2 * REACH + 1, 2)), dma((2 * REACH + 1, 2)), dma((2 * REACH + 1, 2)),
+            dma((2, 2)), dma((2, 2)), dma, dma,
+        ],
+        compiler_params=pltpu.CompilerParams(
+            collective_id=1, has_side_effects=True, vmem_limit_bytes=48 * 2**20
+        ),
+    )(boxes, held_slots, sums)
 
 
 def attend(query_rows, key_rows, value_rows, score_scale):
@@ -71,25 +500,20 @@
     buffer_slot = owners * capacity + jnp.sum(earlier * owner_hits, axis=1)
     targets = (cluster_ids % clusters_here * CLUSTER_SIZE + slots).reshape(-1)
     routing = jnp.full((buffer_rows,), -1, jnp.int32).at[buffer_slot].set(targets)
-    slot_hits = buffer_slot[None, :] == jnp.arange(buffer_rows, dtype=jnp.int32)[:, None]
-    dispatch = jnp.any(slot_hits.reshape(buffer_rows, tok_rows, 2), axis=2).astype(jnp.bfloat16)
-
-    def pack_rows(rows_in):
-        return jnp.dot(dispatch, rows_in, preferred_element_type=jnp.float32).astype(jnp.bfloat16)
-
-    def unpack_rows(rows_in):
-        summed = lax.dot_general(
-            dispatch, rows_in, (((0,), (0,)), ((), ())), preferred_element_type=jnp.float32
-        )
-        return summed.astype(jnp.bfloat16)
-
-    sent_query, sent_key, sent_value, sent_grad, routing_in = (
-        lax.all_to_all(pack_rows(queries), "seq", split_axis=0, concat_axis=0, tiled=True),
-        lax.all_to_all(pack_rows(keys), "seq", split_axis=0, concat_axis=0, tiled=True),
-        lax.all_to_all(pack_rows(values), "seq", split_axis=0, concat_axis=0, tiled=True),
-        lax.all_to_all(pack_rows(out_grad), "seq", split_axis=0, concat_axis=0, tiled=True),
-        lax.all_to_all(routing, "seq", split_axis=0, concat_axis=0, tiled=True),
-    )
+    sent_rows = jnp.concatenate([queries, keys, values, out_grad]).reshape(
+        2, 2 * tok_rows, row_width
+    )
+    copy_slots = buffer_slot.reshape(tok_rows, 2).T
+    slot_rows = jnp.pad(jnp.concatenate([copy_slots, copy_slots], axis=1), ((0, 6), (0, 0)))
+    target_rows = jnp.pad(routing.reshape(shards, 1, capacity), ((0, 0), (0, 0), (0, 120)))
+    arrived, held_slots, held_targets = spread(sent_rows, slot_rows, target_rows)
+    routing_in = held_targets[:, 0, :capacity].reshape(-1)
+
+    def unbox(index):
+        first = index % 2 * capacity
+        return arrived[:, index // 2, first : first + capacity].reshape(buffer_rows, row_width)
+
+    sent_query, sent_key, sent_value, sent_grad = (unbox(i) for i in range(4))
     gather_table = (
         routing_in[None, :] == jnp.arange(cluster_rows, dtype=jnp.int32)[:, None]
     ).astype(jnp.bfloat16)
@@ -111,25 +535,21 @@
     key_rows = gather_rows(sent_key)
     value_rows = gather_rows(sent_value)
     attention, attn_low, attended = attend(query_rows, key_rows, value_rows, score_scale)
-    totals = lax.psum(key_centroids(key_rows), "head")
-    cluster_means = totals * lax.rsqrt(jnp.mean(totals * totals, axis=1, keepdims=True) + 1e-06)
+    sums = jnp.pad(key_centroids(key_rows), ((0, 8 - clusters_here), (0, 0)))
     grad_rows = gather_rows(sent_grad)
     grad_query, grad_key, grad_value = backprop(
         query_rows, key_rows, value_rows, grad_rows, attention, attn_low, score_scale
     )
-    back_out, back_query, back_key, back_value = (
-        lax.all_to_all(scatter_rows(attended), "seq", split_axis=0, concat_axis=0, tiled=True),
-        lax.all_to_all(scatter_rows(grad_query), "seq", split_axis=0, concat_axis=0, tiled=True),
-        lax.all_to_all(scatter_rows(grad_key), "seq", split_axis=0, concat_axis=0, tiled=True),
-        lax.all_to_all(scatter_rows(grad_value), "seq", split_axis=0, concat_axis=0, tiled=True),
-    )
-    return (
-        unpack_rows(back_out),
-        unpack_rows(back_query),
-        unpack_rows(back_key),
-        unpack_rows(back_value),
-        cluster_means,
-    )
+    boxes = jnp.concatenate(
+        [
+            scatter_rows(a).reshape(shards, capacity, row_width)
+            for a in (attended, grad_query, grad_key, grad_value)
+        ],
+        axis=1,
+    ).reshape(shards, 2, 2 * capacity, row_width)
+    rows_back, means = collect(boxes, held_slots, sums)
+    back = rows_back.reshape(4, tok_rows, row_width)
+    return (back[0], back[1], back[2], back[3], means[:clusters_here])
 
 
 def solution(mesh):

time: 549 us -> 352 us (0.64)
  waiting for transfers between devices: 378 us -> 0 us
  Pallas kernels: 0 us -> 310 us
  starting transfers between devices: 87.9 us -> 0 us
  matrix products: 47 us -> 25.4 us
  blocking collectives: 9.32 us -> 0 us
  local copies, waits for them, and re-layouts: 18.6 us -> 11.9 us
    all_to_all x9 -> x0, waiting for transfers between devices: 378 us -> none  [the longest x1 53 us: local(): lax.all_to_all(pack_rows(out_grad), 'seq', split_axis=0, concat_axis=0, t...]
    pallas_call x0 -> x2, Pallas kernels: none -> 310 us  [the longest x1 163 us: spread(): pl.pallas_call(functools.partial(spread_kernel, shards), out_shape=(jax.S...]
    all_to_all x9 -> x0, starting transfers between devices: 87.9 us -> none  [the longest x1 20.4 us: local(): lax.all_to_all(routing, 'seq', split_axis=0, concat_axis=0, tiled=True)]
    dot_general x8 -> x0, matrix products: 13 us -> none  [the longest x4 7.19 us: unpack_rows(): lax.dot_general(dispatch, rows_in, (((0,), (0,)), ((), ())), preferred_el...]
    psum x1 -> x0, blocking collectives: 9.32 us -> none  [local(): totals = lax.psum(key_centroids(key_rows), 'head')]
  transfers between devices with their start and end apart: 9 -> 0, of which waited for: 9 -> 0; matrix products, arithmetic and copies ran while one was open for 11% -> 0% of each run, Pallas kernels for 0% -> 0%
where the time goes in v2:
time: 352 us
  Pallas kernels  310 us (88%)
  matrix products  25.4 us (7%)
  local copies, waits for them, and re-layouts  11.9 us (3%)
  other arithmetic  3.57 us (1%)
    pallas_call x1, Pallas kernels, spread(): pl.pallas_call(functools.partial(spread_kernel, shards), out_shape=(jax.S...  163 us
    pallas_call x1, Pallas kernels, collect(): pl.pallas_call(functools.partial(collect_kernel, shards), out_shape=(jax....  146 us
    dot_general x4, matrix products, gather_rows(): jnp.dot(gather_table, rows_in, preferred_element_type=jnp.float32)  7.93 us

profile of v2, /device:TPU:1, one launch (start us, length us, event | category | flops | bytes accessed | tf_op | source)
XLA Modules:
  0.0 351.6 jit_solution(18275501854094525317)
XLA Ops:
  0.7 0.8 broadcast_multiply_fusion
  3.2 2.4 scatter_custom_fusion
  6.2 163.2 %shard_map.101 = (bf16[128,2,16,512]{3,2,1,0:T(8,128)(2,1)S(1)}, s32[9,8,512]{2,1,0:T(8,128)S(1)}, s32[128,1,128]{2,1,0:T(1,128)S(1)}) custom-call(bf16[2,512,512]{2,1,0:T(8,128)(2,1)S(1)} %bitcast.85, s32[8,512]{1,0:T(8,128)S(1)} %pad.12.slots_ref, s32[128,1,128]{2,1,0:T(1,128)S(1)} %pad.13.targets_ref), custom_call_target="tpu_custom_call" | custom-call | tf_op jit(solution)/shard_map/pallas_call | solution.py:221
  169.4 1.9 copy-done
  171.6 1.9 fusion.37
  173.7 0.3 copy.93
  173.9 1.9 fusion.36
  176.0 0.6 fusion.46
  176.7 0.9 fusion.47
  177.6 0.3 copy.87
  177.9 2.1 fusion.35
  180.0 1.9 fusion.34
  182.2 0.3 copy.90
  182.5 2.2 fusion.99
  184.7 2.1 fusion.39
  186.8 0.3 copy.95
  187.1 1.7 fusion.24
  188.9 0.4 fusion.38
  189.2 0.3 copy.84
  189.5 1.7 fusion.27
  191.3 0.4 fusion.80
  191.7 3.4 fusion.43
  195.1 4.0 %fusion.40 = bf16[2,256,4,128]{1,3,2,0:T(8,128)(2,1)} fusion(bf16[2,256,4,128]{1,3,2,0:T(8,128)(2,1)S(1)} %copy-done.5, f32[2,4,256,256]{2,3,1,0:T(8,128)S(1)} %fusion.80, f32[2,4,256,256]{2,3,1,0:T(8,128)} %get-tuple-element.23, f32[2,4,256]{2,1,0:T(4,128)S(1)} %get-tuple-element.22), kind=kOutput, calls=%fused_computation.41 | convolution fusion | flops 138152192 | bytes 5251072 | tf_op jit(solution)/shard_map/chqk,cqhd->ckhd/dot_general | solution.py:468
  199.1 1.3 copy.92
  200.7 0.8 fusion.26
  201.5 0.8 fusion.25
  202.2 0.4 copy-done.1
  202.7 0.3 copy-done.2
  203.0 0.6 pad_maximum_fusion
  203.6 146.4 %shard_map.102 = (bf16[2,512,512]{2,1,0:T(8,128)(2,1)S(1)}, f32[8,128]{1,0:T(8,128)S(1)}) custom-call(bf16[128,2,16,512]{3,2,1,0:T(8,128)(2,1)S(1)} %bitcast.84, s32[9,8,512]{2,1,0:T(8,128)S(1)} %get-tuple-element.12.held_slots_ref, f32[8,128]{1,0:T(8,128)S(1)} %pad.14.sums_ref), custom_call_target="tpu_custom_call" | custom-call | tf_op jit(solution)/shard_map/pallas_call | solution.py:418
  350.0 1.0 slice_bitcast_fusion
  351.0 0.6 slice.47
  (54 shorter events, 3.2 us)
Async XLA Ops:
  0.6 5.4 %copy-start.6 = (bf16[256,512]{1,0:T(8,128)(2,1)S(1)}, bf16[256,512]{1,0:T(8,128)(2,1)}, u32[]{:S(2)}) copy-start(bf16[256,512]{1,0:T(8,128)(2,1)} %param.9) | copy-start | bytes 786436
  0.6 5.4 %copy-start.7 = (bf16[256,512]{1,0:T(8,128)(2,1)S(1)}, bf16[256,512]{1,0:T(8,128)(2,1)}, u32[]{:S(2)}) copy-start(bf16[256,512]{1,0:T(8,128)(2,1)} %param.8) | copy-start | bytes 786436
  0.7 5.4 %copy-start.8 = (bf16[256,512]{1,0:T(8,128)(2,1)S(1)}, bf16[256,512]{1,0:T(8,128)(2,1)}, u32[]{:S(2)}) copy-start(bf16[256,512]{1,0:T(8,128)(2,1)} %param.7) | copy-start | bytes 786436
  0.7 5.4 %copy-start.9 = (bf16[256,512]{1,0:T(8,128)(2,1)S(1)}, bf16[256,512]{1,0:T(8,128)(2,1)}, u32[]{:S(2)}) copy-start(bf16[256,512]{1,0:T(8,128)(2,1)} %param.6) | copy-start | bytes 786436
  169.4 1.9 copy-start
  177.8 4.6 %copy-start.3 = (bf16[2,256,4,128]{1,3,2,0:T(8,128)(2,1)}, bf16[2,256,4,128]{1,3,2,0:T(8,128)(2,1)S(1)}, u32[]{:S(2)}) copy-start(bf16[2,256,4,128]{1,3,2,0:T(8,128)(2,1)S(1)} %copy.87) | copy-start | bytes 1572868
  182.5 2.2 copy-start.4
  187.1 1.8 copy-start.10
  191.7 3.4 copy-start.5
  201.5 1.2 copy-start.1
  201.5 1.5 copy-start.2

commit v3 on v0

v3 whole, which is shorter than its diff:
```python
import functools
import math

import jax
import jax.numpy as jnp
from jax import lax
from jax.experimental import pallas as pl
from jax.experimental.pallas import tpu as pltpu
from jax.sharding import PartitionSpec as P

HEAD_DIM = 128
CLUSTER_SIZE = 256
RING = 16
HEADS = 4
PEERS = 8
MESH = pl.DeviceIdType.MESH
NEAR_FIRST = (0, 1, -1, 2, -2, 3, -3, 4)
FAR_FIRST = (4, 3, -3, 2, -2, 1, -1, 0)


def place():
    me = lax.axis_index("seq")
    head = lax.axis_index("head")
    return (me, head, me // (2 * RING), lax.rem(me // 2, RING), lax.rem(me, 2))


def device_at(column, height, core):
    return (column * RING + height) * 2 + core


def around(value, size):
    return lax.rem(value + size, size)


def signal(barrier, seq, head):
    pl.semaphore_signal(barrier, inc=1, device_id=(seq, head), device_id_type=MESH)


def remote(source, target, send_sem, recv_sem, seq, head):
    return pltpu.make_async_remote_copy(
        src_ref=source,
        dst_ref=target,
        send_sem=send_sem,
        recv_sem=recv_sem,
        device_id=(seq, head),
        device_id_type=MESH,
    )


def loop(first, last, body):
    def step(index, carry):
        body(index)
        return carry

    lax.fori_loop(first, last, step, 0)


def hit_table(first_row, second_row, head):
    shape = (512, 512)
    row = lax.broadcasted_iota(jnp.int32, shape, 0)
    lane = lax.broadcasted_iota(jnp.int32, shape, 1)
    peer = row // 64
    device = ((peer // 2) * HEADS + head) * 2 + peer % 2
    wanted = (device * 4 + row // 16 % 4) * 8 + row % 8
    half = shape[1] // 2
    copies = [
        jnp.concatenate([first_row[:, c * half : (c + 1) * half], second_row[:, c * half : (c + 1) * half]], axis=1)
        for c in range(2)
    ]
    hit = (copies[0] == wanted) | (copies[1] == wanted)
    same = row // 8 % 2 == lane // half
    return jnp.where(hit & same, 1.0, 0.0).astype(jnp.bfloat16)


def spread_kernel(
    shards, rows_ref, slots_ref, lines_ref, boxes_ref, held_slots_ref, held_lines_ref,
    full, packed, slot_send, slot_recv, line_send, line_recv,
    z_send, z_recv, y_send, y_recv, x_send, x_recv, own_sem,
):
    me, head, column, height, core = place()
    mine = column * 2 + core
    here = lax.rem(height, HEADS) == head
    barrier = pltpu.get_barrier_semaphore()
    loop(1, shards, lambda step: signal(barrier, lax.rem(me + step, shards), head))
    for step in (1, HEADS - 1):
        signal(barrier, me, lax.rem(head + step, HEADS))

    def greet_source(source):
        @pl.when(jnp.logical_not(here & (source == height)))
        def _():
            signal(barrier, device_at(column, source, core), lax.rem(height, HEADS))

    loop(0, RING, greet_source)
    held_slots_ref[height] = slots_ref[...]
    held_lines_ref[me] = lines_ref[mine]
    pl.semaphore_wait(barrier, shards - 1 + 2 + RING - jnp.where(here, 1, 0))

    def send_slots(step):
        peer = device_at(column, lax.rem(height + step, RING), core)
        remote(slots_ref, held_slots_ref.at[height], slot_send, slot_recv, peer, head).start()

    loop(1, RING, send_slots)

    def send_quarter(index):
        turn = lax.rem(index // 4, 4)
        quad = lax.rem(height // 4 + jnp.where(turn == 2, 3, jnp.where(turn == 3, 2, turn)), 4)
        quarter = lax.rem(head + index, HEADS)
        plane = 4 * quad + head
        source = rows_ref.at[quad, pl.ds(pl.multiple_of(quarter * 64, 64), 64)]
        target = full.at[height, quarter]
        stays = (plane == height) & (quarter == head)

        @pl.when(stays)
        def _():
            pltpu.make_async_copy(source, target, z_recv.at[height]).start()

        @pl.when(jnp.logical_not(stays))
        def _():
            remote(
                source, target, z_send, z_recv.at[height],
                device_at(column, plane, core), quarter,
            ).start()

    loop(0, RING, send_quarter)

    def send_line(step):
        peer = lax.rem(me + step, shards)
        peer_column = peer // (2 * RING) * 2 + lax.rem(peer, 2)
        remote(
            lines_ref.at[peer_column], held_lines_ref.at[me], line_send, line_recv, peer, head
        ).start()

    loop(1, shards, send_line)

    def y_copy(source, quarter, step, kind):
        part = full.at[source, around(quarter, HEADS)]
        return remote(
            part, part, y_send, y_recv.at[kind, source], me, around(head + step, HEADS)
        )

    def pair_at(turn):
        return lax.rem(height // 2 + NEAR_FIRST[turn] + 8, 8)

    def share(turn):
        for side in range(2):
            source = pair_at(turn) * 2 + side
            part = full.at[source, head]
            remote(part, part, z_send, z_recv.at[source], me, head).wait_recv()
            y_copy(source, head, 1, 0).start()
            y_copy(source, head, -1, 1).start()

    def relay(turn):
        for side in range(2):
            source = pair_at(turn) * 2 + side
            if side == 0:
                y_copy(source, head - 1, 1, 0).wait_recv()
                y_copy(source, head - 1, 1, 2).start()
                y_copy(source, head + 1, -1, 1).wait_recv()
            else:
                y_copy(source, head + 1, -1, 1).wait_recv()
                y_copy(source, head + 1, -1, 2).start()
                y_copy(source, head - 1, 1, 0).wait_recv()

    def deliver(turn):
        pair = pair_at(turn)
        for side in range(2):
            y_copy(pair * 2 + side, head + 2, 1, 2).wait_recv()
        table = hit_table(held_slots_ref[pair * 2], held_slots_ref[pair * 2 + 1], head)
        tokens = full[pl.ds(pair * 2, 2)].reshape(512, 512)
        result = jnp.dot(table, tokens, preferred_element_type=jnp.float32)
        packed[turn] = result.astype(jnp.bfloat16).reshape(PEERS, 64, 512)
        target = boxes_ref.at[mine * 8 + pair]
        pltpu.make_async_copy(packed.at[turn, mine], target, own_sem.at[turn]).start()

        def send(step):
            peer = lax.rem(mine + step, PEERS)
            remote(
                packed.at[turn, peer], target, x_send, x_recv,
                device_at(peer // 2, height, lax.rem(peer, 2)), head,
            ).start()

        loop(1, PEERS, send)

    other = lax.rem(head + 1, HEADS)
    for turn in range(10):
        if turn < 8:
            share(turn)
        if 1 <= turn < 9:
            relay(turn - 1)
        if turn == 2:
            lot = held_slots_ref.at[pl.ds(0, RING - 1)]
            remote(lot, lot, slot_send, slot_recv, me, other).wait()
        if turn >= 2:
            deliver(turn - 2)
    for turn in range(8):
        pltpu.make_async_copy(
            packed.at[turn, mine], boxes_ref.at[mine * 8 + turn], own_sem.at[turn]
        ).wait()
    lot = boxes_ref.at[pl.ds(0, 56)]
    remote(lot, lot, x_send, x_recv, me, other).wait()
    lot = held_lines_ref.at[pl.ds(0, shards - 1)]
    remote(lot, lot, line_send, line_recv, me, other).wait()
    lot = full.at[pl.ds(0, 12)]
    remote(lot, lot, y_send, y_recv.at[0, 0], me, other).wait_send()

    def sent_quarter(index):
        part = full.at[0, 0]
        remote(part, part, z_send, z_recv.at[0], me, other).wait_send()

    loop(0, RING - jnp.where(here, 1, 0), sent_quarter)


def spread(rows, slots, lines, shards):
    vmem = pl.BlockSpec(memory_space=pltpu.VMEM)
    dma = pltpu.SemaphoreType.DMA
    return pl.pallas_call(
        functools.partial(spread_kernel, shards),
        out_shape=(
            jax.ShapeDtypeStruct((64, 64, 512), jnp.bfloat16),
            jax.ShapeDtypeStruct((RING,) + slots.shape, jnp.int32),
            jax.ShapeDtypeStruct((shards,) + lines.shape[1:], jnp.int32),
        ),
        in_specs=[vmem] * 3,
        out_specs=(vmem,) * 3,
        scratch_shapes=[
            pltpu.VMEM((RING, 4, 64, 512), jnp.bfloat16),
            pltpu.VMEM((8, PEERS, 64, 512), jnp.bfloat16),
            dma, dma, dma, dma,
            dma, dma((RING,)), dma, dma((3, RING)), dma, dma, dma((8,)),
        ],
        compiler_params=pltpu.CompilerParams(
            collective_id=0, has_side_effects=True, vmem_limit_bytes=48 * 2**20
        ),
    )(rows, slots, lines)


def collect_kernel(
    boxes_ref, held_slots_ref, sums_ref, rows_ref, means_ref,
    held, part, far, near, done, sums, x_send, x_recv, own_sem,
    y_send, far_recv, near_recv, z_send, z_recv, sum_send, sum_recv,
):
    me, head, column, height, core = place()
    mine = column * 2 + core
    here = lax.rem(height, HEADS) == head
    owner = (height // 4 == head) & (lax.rem(height // 2, 2) == core)
    barrier = pltpu.get_barrier_semaphore()

    def greet_peer(step):
        peer = lax.rem(mine + step, PEERS)
        signal(barrier, device_at(peer // 2, height, lax.rem(peer, 2)), head)

    loop(1, PEERS, greet_peer)
    for step in (1, HEADS - 1):
        signal(barrier, me, lax.rem(head + step, HEADS))

    def greet_relay(index):
        plane = index // 4 * 4 + head
        quarter = lax.rem(index, 4)

        @pl.when(jnp.logical_not((plane == height) & (quarter == head)))
        def _():
            signal(barrier, device_at(column, plane, core), quarter)

    loop(0, RING, greet_relay)

    def greet_summer(plane):
        @pl.when(jnp.logical_not(owner & (plane == height)))
        def _():
            signal(barrier, device_at(column, plane, lax.rem(height // 2, 2)), height // 4)

    loop(0, RING, greet_summer)
    pl.semaphore_wait(
        barrier, PEERS - 1 + 2 + 2 * RING - jnp.where(here, 1, 0) - jnp.where(owner, 1, 0)
    )

    def pair_at(turn):
        return lax.rem(height // 2 + FAR_FIRST[turn] + 8, 8)

    for turn in range(8):
        pair = pair_at(turn)
        pltpu.make_async_copy(
            boxes_ref.at[mine * 8 + pair], held.at[pair, mine], own_sem.at[turn]
        ).start()

        def send_box(step):
            peer = lax.rem(mine + step, PEERS)
            remote(
                boxes_ref.at[peer * 8 + pair], held.at[pair, mine], x_send, x_recv.at[pair],
                device_at(peer // 2, height, lax.rem(peer, 2)), head,
            ).start()

        loop(1, PEERS, send_box)

    def send_sum(index):
        group = index // 4
        there = lax.rem(head + index, HEADS)
        peer = device_at(column, (head * 2 + core) * 2 + group // 2, lax.rem(group, 2))
        stays = (peer == me) & (there == head)

        @pl.when(stays)
        def _():
            pltpu.make_async_copy(sums_ref.at[group], sums.at[height], sum_recv).start()

        @pl.when(jnp.logical_not(stays))
        def _():
            remote(
                sums_ref.at[group], sums.at[height], sum_send, sum_recv, peer, there
            ).start()

    loop(0, RING, send_sum)

    def up(source, quarter, target, recv):
        return remote(
            part.at[source, around(quarter, HEADS)], target, y_send, recv, me,
            around(head + 1, HEADS),
        )

    def down(source, quarter, target, recv):
        return remote(
            part.at[source, around(quarter, HEADS)], target, y_send, recv, me,
            around(head - 1, HEADS),
        )

    def unpack(turn):
        pair = pair_at(turn)
        pltpu.make_async_copy(
            boxes_ref.at[mine * 8 + pair], held.at[pair, mine], own_sem.at[turn]
        ).wait()
        lot = held.at[pair, pl.ds(0, PEERS - 1)]
        remote(lot, lot, x_send, x_recv.at[pair], me, around(head + 1, HEADS)).wait_recv()
        table = hit_table(held_slots_ref[pair * 2], held_slots_ref[pair * 2 + 1], head)
        result = lax.dot_general(
            table, held[pair].reshape(512, 512), (((0,), (0,)), ((), ())),
            preferred_element_type=jnp.float32,
        )
        part[pl.ds(pair * 2, 2)] = result.astype(jnp.bfloat16).reshape(2, 4, 64, 512)
        even, odd = (pair * 2, pair * 2 + 1)
        up(even, head + 2, far.at[even], far_recv.at[even]).start()
        down(even, head - 1, near.at[1, even], near_recv.at[1, even]).start()
        down(odd, head + 2, far.at[odd], far_recv.at[odd]).start()
        up(odd, head + 1, near.at[0, odd], near_recv.at[0, odd]).start()

    def join(turn):
        even = pair_at(turn) * 2
        for source, step in ((even, 1), (even + 1, -1)):
            spot = around(head + step, HEADS)
            up(source, head + step, far.at[source], far_recv.at[source]).wait_recv()
            total = part[source, spot].astype(jnp.float32) + far[source].astype(jnp.float32)
            part[source, spot] = total.astype(jnp.bfloat16)
            if step == 1:
                up(source, head + 1, near.at[0, source], near_recv.at[0, source]).start()
            else:
                down(source, head - 1, near.at[1, source], near_recv.at[1, source]).start()

    def finish(turn):
        for side in range(2):
            source = pair_at(turn) * 2 + side
            total = part[source, head].astype(jnp.float32)
            for way in range(2):
                up(source, head, near.at[way, source], near_recv.at[way, source]).wait_recv()
                total += near[way, source].astype(jnp.float32)
            done[source] = total.astype(jnp.bfloat16)
            target = rows_ref.at[height // 4, head]
            stays = here & (source == height)

            @pl.when(stays)
            def _():
                pltpu.make_async_copy(done.at[source], target, z_recv).start()

            @pl.when(jnp.logical_not(stays))
            def _():
                remote(
                    done.at[source], target, z_send, z_recv,
                    device_at(column, source, core), lax.rem(height, HEADS),
                ).start()

    for turn in range(10):
        if turn < 8:
            unpack(turn)
        if 1 <= turn < 9:
            join(turn - 1)
        if turn >= 2:
            finish(turn - 2)
    other = around(head + 1, HEADS)
    remote(sums, sums, sum_send, sum_recv, me, other).wait_recv()
    grand = sums[0]
    for plane in range(1, RING):
        grand += sums[plane]
    means_ref[...] = grand * lax.rsqrt(jnp.mean(grand * grand, axis=1, keepdims=True) + 1e-06)
    lot = boxes_ref.at[pl.ds(0, 56)]
    remote(lot, lot, x_send, x_recv.at[0], me, other).wait_send()
    lot = part.at[pl.ds(0, 12)]
    remote(lot, lot, y_send, far_recv.at[0], me, other).wait_send()

    def sent_sum(index):
        remote(sums.at[0], sums.at[0], sum_send, sum_recv, me, other).wait_send()

    loop(0, RING - jnp.where(owner, 1, 0), sent_sum)

    def sent_rows(index):
        remote(done.at[0], done.at[0], z_send, z_recv, me, other).wait_send()

    loop(0, RING - jnp.where(here, 1, 0), sent_rows)
    remote(rows_ref, rows_ref, z_send, z_recv, me, other).wait_recv()


def collect(boxes, held_slots, sums):
    vmem = pl.BlockSpec(memory_space=pltpu.VMEM)
    dma = pltpu.SemaphoreType.DMA
    return pl.pallas_call(
        collect_kernel,
        out_shape=(
            jax.ShapeDtypeStruct((4, 4, 64, 512), jnp.bfloat16),
            jax.ShapeDtypeStruct(sums.shape[1:], jnp.float32),
        ),
        in_specs=[vmem] * 3,
        out_specs=(vmem,) * 2,
        scratch_shapes=[
            pltpu.VMEM((8, PEERS, 64, 512), jnp.bfloat16),
            pltpu.VMEM((RING, 4, 64, 512), jnp.bfloat16),
            pltpu.VMEM((RING, 64, 512), jnp.bfloat16),
            pltpu.VMEM((2, RING, 64, 512), jnp.bfloat16),
            pltpu.VMEM((RING, 64, 512), jnp.bfloat16),
            pltpu.VMEM((RING,) + sums.shape[1:], jnp.float32),
            dma, dma((8,)), dma((8,)),
            dma, dma((RING,)), dma((2, RING)), dma, dma, dma, dma,
        ],
        compiler_params=pltpu.CompilerParams(
            collective_id=1, has_side_effects=True, vmem_limit_bytes=48 * 2**20
        ),
    )(boxes, held_slots, sums)


def attend(query_rows, key_rows, value_rows, score_scale):
    scores = (
        jnp.einsum("cqhd,ckhd->chqk", query_rows, key_rows, preferred_element_type=jnp.float32)
        * score_scale
    )
    slot_order = jnp.arange(query_rows.shape[1], dtype=jnp.int32)
    allowed = slot_order[None, :] <= slot_order[:, None]
    scores = jnp.where(allowed, scores, jnp.float32(-1e30))
    row_max = jnp.max(scores, axis=3, keepdims=True)
    weights = jnp.exp(scores - row_max)
    attention = weights / jnp.sum(weights, axis=3, keepdims=True)
    attn_low = attention.astype(jnp.bfloat16)
    attended = jnp.einsum(
        "chqk,ckhd->cqhd", attn_low, value_rows, preferred_element_type=jnp.float32
    )
    return (attention, attn_low, attended.astype(jnp.bfloat16))


def backprop(query_rows, key_rows, value_rows, grad_rows, attention, attn_low, score_scale):
    prob_grad = jnp.einsum(
        "cqhd,ckhd->chqk", grad_rows, value_rows, preferred_element_type=jnp.float32
    )
    row_dot = jnp.sum(attention * prob_grad, axis=3, keepdims=True)
    grad_score = (attention * (prob_grad - row_dot) * score_scale).astype(jnp.bfloat16)
    grad_query = jnp.einsum(
        "chqk,ckhd->cqhd", grad_score, key_rows, preferred_element_type=jnp.float32
    )
    grad_key = jnp.einsum(
        "chqk,cqhd->ckhd", grad_score, query_rows, preferred_element_type=jnp.float32
    )
    grad_value = jnp.einsum(
        "chqk,cqhd->ckhd", attn_low, grad_rows, preferred_element_type=jnp.float32
    )
    return (
        grad_query.astype(jnp.bfloat16),
        grad_key.astype(jnp.bfloat16),
        grad_value.astype(jnp.bfloat16),
    )


def key_centroids(key_rows):
    key_float = key_rows.astype(jnp.float32)
    normed = key_float * lax.rsqrt(jnp.mean(key_float * key_float, axis=3, keepdims=True) + 1e-06)
    return jnp.sum(normed, axis=(1, 2))


def local(queries, keys, values, out_grad, cluster_ids, slots):
    tok_rows = queries.shape[0]
    shards = lax.axis_size("seq")
    score_scale = 1.0 / math.sqrt(HEAD_DIM)
    groups = (cluster_ids // 2).reshape(-1)
    group_hits = (groups[:, None] == jnp.arange(shards, dtype=jnp.int32)[None, :]).astype(jnp.int32)
    earlier = jnp.cumsum(group_hits, axis=0) - group_hits
    buffer_slot = groups * 8 + jnp.sum(earlier * group_hits, axis=1)
    targets = (cluster_ids % 2 * CLUSTER_SIZE + slots).reshape(-1)
    routing = jnp.full((shards * 8,), -1, jnp.int32).at[buffer_slot].set(targets)
    lines = lax.dynamic_index_in_dim(
        routing.reshape(4, HEADS, 2, 32), lax.axis_index("head"), axis=1, keepdims=False
    )
    lines = jnp.pad(lines.reshape(PEERS, 1, 32), ((0, 0), (0, 0), (0, 96)))
    slot_row = buffer_slot.reshape(tok_rows, 2).T.reshape(1, 2 * tok_rows)

    def by_head(rows_in):
        return rows_in.reshape(tok_rows, HEADS, HEAD_DIM).transpose(1, 0, 2)

    sent = jnp.concatenate([by_head(a) for a in (queries, keys, values, out_grad)], axis=2)
    arrived, held_slots, held_lines = spread(sent, slot_row, lines, shards)
    routing_in = (
        held_lines[:, 0, :32]
        .reshape(4, 8, 2, 2, 4, 8)
        .transpose(4, 0, 3, 1, 2, 5)
        .reshape(4, 1024)
    )
    gather_table = (
        routing_in[:, None, :] == jnp.arange(512, dtype=jnp.int32)[None, :, None]
    ).astype(jnp.bfloat16)
    arrived = arrived.reshape(64, 4, 16, 512).transpose(1, 0, 2, 3).reshape(4, 1024, 512)
    grouped = jnp.einsum(
        "grs,gsd->grd", gather_table, arrived, preferred_element_type=jnp.float32
    ).astype(jnp.bfloat16)
    query_rows, key_rows, value_rows, grad_rows = (
        grouped[:, :, i * HEAD_DIM : (i + 1) * HEAD_DIM].reshape(8, CLUSTER_SIZE, 1, HEAD_DIM)
        for i in range(4)
    )
    attention, attn_low, attended = attend(query_rows, key_rows, value_rows, score_scale)
    sums = jnp.pad(key_centroids(key_rows).reshape(4, 2, HEAD_DIM), ((0, 0), (0, 6), (0, 0)))
    grads = backprop(
        query_rows, key_rows, value_rows, grad_rows, attention, attn_low, score_scale
    )
    results = jnp.concatenate([a.reshape(4, 512, HEAD_DIM) for a in (attended,) + grads], axis=2)
    boxes = jnp.einsum(
        "grs,grd->gsd", gather_table, results, preferred_element_type=jnp.float32
    ).astype(jnp.bfloat16)
    boxes = boxes.reshape(4, 64, 16, 512).transpose(1, 0, 2, 3).reshape(64, 64, 512)
    rows_back, means = collect(boxes, held_slots, sums)
    back = rows_back.reshape(HEADS, tok_rows, 4, HEAD_DIM)
    outs = tuple(
        back[:, :, i].transpose(1, 0, 2).reshape(tok_rows, HEADS * HEAD_DIM) for i in range(4)
    )
    return outs + (means[:2],)


def solution(mesh):
    placed = (
        P("seq", "head"),
        P("seq", "head"),
        P("seq", "head"),
        P("seq", "head"),
        P("seq", None),
        P("seq", None),
    )
    return jax.shard_map(
        local,
        mesh=mesh,
        in_specs=placed,
        out_specs=(
            P("seq", "head"),
            P("seq", "head"),
            P("seq", "head"),
            P("seq", "head"),
            P("seq", None),
        ),
        check_vma=False,
    )
```

time: 549 us -> 268 us (0.49)
  waiting for transfers between devices: 378 us -> 0 us
  Pallas kernels: 0 us -> 212 us
  starting transfers between devices: 87.9 us -> 0 us
  matrix products: 47 us -> 23.9 us
  blocking collectives: 9.32 us -> 0 us
    all_to_all x9 -> x0, waiting for transfers between devices: 378 us -> none  [the longest x1 53 us: local(): lax.all_to_all(pack_rows(out_grad), 'seq', split_axis=0, concat_axis=0, t...]
    pallas_call x0 -> x2, Pallas kernels: none -> 212 us  [the longest x1 132 us: spread(): pl.pallas_call(functools.partial(spread_kernel, shards), out_shape=(jax.S...]
    all_to_all x9 -> x0, starting transfers between devices: 87.9 us -> none  [the longest x1 20.4 us: local(): lax.all_to_all(routing, 'seq', split_axis=0, concat_axis=0, tiled=True)]
    dot_general x16 -> x2, matrix products: 29 us -> 8.23 us  [the longest x1 4.91 us: local(): jnp.einsum('grs,gsd->grd', gather_table, arrived, preferred_element_type=...]
    psum x1 -> x0, blocking collectives: 9.32 us -> none  [local(): totals = lax.psum(key_centroids(key_rows), 'head')]
  transfers between devices with their start and end apart: 9 -> 0, of which waited for: 9 -> 0; matrix products, arithmetic and copies ran while one was open for 11% -> 0% of each run, Pallas kernels for 0% -> 0%
where the time goes in v3:
time: 268 us; the launch traced here: 263 us
  Pallas kernels  212 us (79%)
  matrix products  23.9 us (9%)
  local copies, waits for them, and re-layouts  22.5 us (8%)
  other arithmetic  3.8 us (1%)
    pallas_call x1, Pallas kernels, spread(): pl.pallas_call(functools.partial(spread_kernel, shards), out_shape=(jax.S...  132 us
    pallas_call x1, Pallas kernels, collect(): pl.pallas_call(collect_kernel, out_shape=(jax.ShapeDtypeStruct((4, 4, 64,...  79.9 us
    unnamed x26, local copies, waits for them, and re-layouts  5.59 us

profile of v3, /device:TPU:1, one launch (start us, length us, event | category | flops | bytes accessed | tf_op | source)
XLA Modules:
  0.0 263.2 jit_solution(14030504881477591830)
XLA Ops:
  0.6 0.7 broadcast_compare_fusion
  1.6 0.8 copy.83
  2.4 0.8 copy.73
  4.7 2.4 scatter_custom_fusion
  9.0 132.0 %shard_map.101 = (bf16[64,64,512]{2,1,0:T(8,128)(2,1)S(1)}, s32[16,1,512]{2,1,0:T(1,128)S(1)}, s32[128,1,128]{2,1,0:T(1,128)S(1)}) custom-call(bf16[4,256,512]{2,1,0:T(8,128)(2,1)S(1)} %pad_maximum_fusion.rows_ref, s32[1,512]{1,0:T(1,128)S(1)} %bitcast.102, s32[8,1,128]{2,1,0:T(1,128)S(1)} %pad.8.lines_ref), custom_call_target="tpu_custom_call" | custom-call | tf_op jit(solution)/shard_map/pallas_call | solution.py:216
  141.2 2.5 copy.85
  144.0 0.4 eq.50
  144.4 4.9 %fusion.17 = bf16[4,512,512]{2,1,0:T(8,128)(2,1)S(1)} fusion(bf16[4,1024,512]{2,1,0:T(8,128)(2,1)} %bitcast.104, s32[4,1024]{1,0:T(4,128)S(1)} %eq.50), kind=kOutput, calls=%fused_computation.21 | convolution fusion | flops 2150629376 | bytes 6307840 | tf_op jit(solution)/shard_map/grs,gsd->grd/dot_general | solution.py:511
  149.3 0.4 multiply_reduce_fusion.2
  149.7 1.6 slice_convert_fusion
  151.2 0.3 multiply_reduce_fusion.1
  151.6 3.4 %fusion.67 = (f32[8,256]{1,0:T(8,128)S(1)}, f32[8,256,256]{1,2,0:T(8,128)}) fusion(pred[256,256]{0,1:T(8,128)(4,1)S(1)} %iota_compare_fusion.7, bf16[8,256,128]{2,1,0:T(8,128)(2,1)} %bitcast.125, bf16[8,256,128]{2,1,0:T(8,128)(2,1)} %bitcast.127), kind=kOutput, calls=%fused_computation.84 | convolution fusion | flops 136315136 | bytes 3219456 | tf_op jit(solution)/shard_map/sub | solution.py:443
  154.9 2.1 fusion.32
  157.0 1.0 copy.98
  158.0 1.9 fusion.31
  160.0 1.0 copy.89
  161.0 0.4 fusion.68
  161.4 4.0 %fusion.36 = bf16[8,256,1,128]{1,3,0,2:T(8,128)(2,1)} fusion(bf16[8,256,128]{2,1,0:T(8,128)(2,1)} %bitcast.128, f32[8,256,256]{1,2,0:T(8,128)S(1)} %fusion.68, f32[8,256,256]{1,2,0:T(8,128)} %get-tuple-element.33, f32[8,256]{1,0:T(8,128)S(1)} %get-tuple-element.32), kind=kOutput, calls=%fused_computation.32 | convolution fusion | flops 138152192 | bytes 5251072 | tf_op jit(solution)/shard_map/chqk,ckhd->cqhd/dot_general | solution.py:458
  165.5 3.9 %fusion.33 = bf16[8,256,1,128]{1,3,0,2:T(8,128)(2,1)} fusion(bf16[8,256,128]{2,1,0:T(8,128)(2,1)S(1)} %bitcast.126, f32[8,256,256]{1,2,0:T(8,128)S(1)} %fusion.68, f32[8,256,256]{1,2,0:T(8,128)} %get-tuple-element.33, f32[8,256]{1,0:T(8,128)S(1)} %get-tuple-element.32), kind=kOutput, calls=%fused_computation.31 | convolution fusion | flops 138152192 | bytes 5251072 | tf_op jit(solution)/shard_map/chqk,cqhd->ckhd/dot_general | solution.py:461
  169.3 1.4 copy.95
  170.7 1.3 copy.92
  172.1 3.3 %fusion.6 = bf16[4,1024,512]{2,1,0:T(8,128)(2,1)S(1)} fusion(s32[4,1024]{1,0:T(4,128)S(1)} %eq.50, bf16[4,512,128]{2,1,0:T(8,128)(2,1)S(1)} %bitcast.129, bf16[4,512,128]{2,1,0:T(8,128)(2,1)S(1)} %bitcast.131, bf16[4,512,128]{2,1,0:T(8,128)(2,1)S(1)} %bitcast.132, bf16[4,512,128]{2,1,0:T(8,128)(2,1)S(1)} %bitcast.130), kind=kOutput, calls=%fused_computation.8 | convolution fusion | flops 2160066560 | bytes 6307840 | tf_op jit(solution)/shard_map/grs,grd->gsd/dot_general | solution.py:524
  175.4 0.6 copy.99
  176.1 79.9 %shard_map.102 = (bf16[4,4,64,512]{3,2,1,0:T(8,128)(2,1)S(1)}, f32[8,128]{1,0:T(8,128)S(1)}) custom-call(bf16[64,64,512]{2,1,0:T(8,128)(2,1)S(1)} %bitcast.100, s32[16,1,512]{2,1,0:T(1,128)S(1)} %get-tuple-element.12.held_slots_ref, f32[4,8,128]{2,1,0:T(8,128)S(1)} %pad.9.sums_ref), custom_call_target="tpu_custom_call" | custom-call | tf_op jit(solution)/shard_map/pallas_call | solution.py:410
  256.3 0.6 slice.47
  256.8 1.6 fusion.66
  258.4 0.4 copy.134
  258.8 0.8 copy.111
  259.6 0.3 copy.133
  260.0 0.8 copy.110
  261.2 0.8 copy.109
  262.4 0.8 copy.108
  (56 shorter events, 4.8 us)
Async XLA Ops:
  0.6 6.9 %copy-start.3 = (bf16[256,512]{1,0:T(8,128)(2,1)S(1)}, bf16[256,512]{1,0:T(8,128)(2,1)}, u32[]{:S(2)}) copy-start(bf16[256,512]{1,0:T(8,128)(2,1)} %param.6) | copy-start | bytes 786436
  3.4 4.4 %copy-start.4 = (bf16[256,512]{1,0:T(8,128)(2,1)S(1)}, bf16[256,512]{1,0:T(8,128)(2,1)}, u32[]{:S(2)}) copy-start(bf16[256,512]{1,0:T(8,128)(2,1)} %param.7) | copy-start | bytes 786436
  4.3 3.9 %copy-start.5 = (bf16[256,512]{1,0:T(8,128)(2,1)S(1)}, bf16[256,512]{1,0:T(8,128)(2,1)}, u32[]{:S(2)}) copy-start(bf16[256,512]{1,0:T(8,128)(2,1)} %param.8) | copy-start | bytes 786436
  4.4 4.1 %copy-start.6 = (bf16[256,512]{1,0:T(8,128)(2,1)S(1)}, bf16[256,512]{1,0:T(8,128)(2,1)}, u32[]{:S(2)}) copy-start(bf16[256,512]{1,0:T(8,128)(2,1)} %param.9) | copy-start | bytes 786436
  161.4 4.1 %copy-start = (bf16[4,512,128]{2,1,0:T(8,128)(2,1)S(1)}, bf16[4,512,128]{2,1,0:T(8,128)(2,1)}, u32[]{:S(2)}) copy-start(bf16[4,512,128]{2,1,0:T(8,128)(2,1)} %get-tuple-element.25) | copy-start | bytes 1572868
  169.3 2.7 %copy-start.1 = (bf16[8,256,1,128]{3,1,0,2:T(8,128)(2,1)S(1)}, bf16[8,256,1,128]{3,1,0,2:T(8,128)(2,1)}, u32[]{:S(2)}) copy-start(bf16[8,256,1,128]{3,1,0,2:T(8,128)(2,1)} %copy.98) | copy-start | bytes 1572868
  169.3 2.7 %copy-start.2 = (bf16[8,256,1,128]{3,1,0,2:T(8,128)(2,1)S(1)}, bf16[8,256,1,128]{3,1,0,2:T(8,128)(2,1)}, u32[]{:S(2)}) copy-start(bf16[8,256,1,128]{3,1,0,2:T(8,128)(2,1)} %copy.89) | copy-start | bytes 1572868

commit v4 on v3

--- a/solution.py
+++ b/solution.py
@@ -14,8 +14,9 @@
 HEADS = 4
 PEERS = 8
 MESH = pl.DeviceIdType.MESH
-NEAR_FIRST = (0, 1, -1, 2, -2, 3, -3, 4)
-FAR_FIRST = (4, 3, -3, 2, -2, 1, -1, 0)
+OUTWARD = (0, 1, 4, -3, -2, 3, 2, -1)
+RETURN = (4, 3, -2, -3, 2, 1, 0, -1)
+AHEAD = 3
 
 
 def place():
@@ -55,82 +56,102 @@
     lax.fori_loop(first, last, step, 0)
 
 
-def hit_table(first_row, second_row, head):
+def hit_table(notes_ref, pair, head):
     shape = (512, 512)
     row = lax.broadcasted_iota(jnp.int32, shape, 0)
     lane = lax.broadcasted_iota(jnp.int32, shape, 1)
     peer = row // 64
     device = ((peer // 2) * HEADS + head) * 2 + peer % 2
     wanted = (device * 4 + row // 16 % 4) * 8 + row % 8
-    half = shape[1] // 2
     copies = [
-        jnp.concatenate([first_row[:, c * half : (c + 1) * half], second_row[:, c * half : (c + 1) * half]], axis=1)
+        jnp.concatenate(
+            [notes_ref[pair * 2 + side, 2 * c + part] for side in range(2) for part in range(2)],
+            axis=1,
+        )
         for c in range(2)
     ]
     hit = (copies[0] == wanted) | (copies[1] == wanted)
-    same = row // 8 % 2 == lane // half
+    same = row // 8 % 2 == lane // 256
     return jnp.where(hit & same, 1.0, 0.0).astype(jnp.bfloat16)
 
 
 def spread_kernel(
-    shards, rows_ref, slots_ref, lines_ref, boxes_ref, held_slots_ref, held_lines_ref,
-    full, packed, slot_send, slot_recv, line_send, line_recv,
-    z_send, z_recv, y_send, y_recv, x_send, x_recv, own_sem,
+    rows_ref, notes_ref, boxes_ref, held_notes_ref, lines_ref,
+    spread_rows, full, packed, note_send, note_recv, line_send, line_recv, line_own,
+    first_send, first_recv, stay_sem, z_send, z_recv, y_send, y_recv, x_send, x_recv, own_sem,
 ):
     me, head, column, height, core = place()
     mine = column * 2 + core
-    here = lax.rem(height, HEADS) == head
     barrier = pltpu.get_barrier_semaphore()
-    loop(1, shards, lambda step: signal(barrier, lax.rem(me + step, shards), head))
-    for step in (1, HEADS - 1):
+
+    def greet_ring(step):
+        signal(barrier, device_at(column, lax.rem(height + step, RING), core), head)
+
+    loop(1, RING, greet_ring)
+
+    def greet_peer(step):
+        peer = lax.rem(mine + step, PEERS)
+        signal(barrier, device_at(peer // 2, height, lax.rem(peer, 2)), head)
+
+    loop(1, PEERS, greet_peer)
+    for step in range(1, HEADS):
         signal(barrier, me, lax.rem(head + step, HEADS))
-
-    def greet_source(source):
-        @pl.when(jnp.logical_not(here & (source == height)))
-        def _():
-            signal(barrier, device_at(column, source, core), lax.rem(height, HEADS))
-
-    loop(0, RING, greet_source)
-    held_slots_ref[height] = slots_ref[...]
-    held_lines_ref[me] = lines_ref[mine]
-    pl.semaphore_wait(barrier, shards - 1 + 2 + RING - jnp.where(here, 1, 0))
-
-    def send_slots(step):
+    other = lax.rem(head + 1, HEADS)
+    held_notes_ref[height] = notes_ref[...]
+    pl.semaphore_wait(barrier, RING - 1 + PEERS - 1 + HEADS - 1)
+
+    def send_notes(step):
         peer = device_at(column, lax.rem(height + step, RING), core)
-        remote(slots_ref, held_slots_ref.at[height], slot_send, slot_recv, peer, head).start()
-
-    loop(1, RING, send_slots)
-
-    def send_quarter(index):
-        turn = lax.rem(index // 4, 4)
-        quad = lax.rem(height // 4 + jnp.where(turn == 2, 3, jnp.where(turn == 3, 2, turn)), 4)
-        quarter = lax.rem(head + index, HEADS)
-        plane = 4 * quad + head
-        source = rows_ref.at[quad, pl.ds(pl.multiple_of(quarter * 64, 64), 64)]
-        target = full.at[height, quarter]
-        stays = (plane == height) & (quarter == head)
-
-        @pl.when(stays)
-        def _():
-            pltpu.make_async_copy(source, target, z_recv.at[height]).start()
-
-        @pl.when(jnp.logical_not(stays))
-        def _():
-            remote(
-                source, target, z_send, z_recv.at[height],
-                device_at(column, plane, core), quarter,
-            ).start()
-
-    loop(0, RING, send_quarter)
-
-    def send_line(step):
-        peer = lax.rem(me + step, shards)
-        peer_column = peer // (2 * RING) * 2 + lax.rem(peer, 2)
-        remote(
-            lines_ref.at[peer_column], held_lines_ref.at[me], line_send, line_recv, peer, head
-        ).start()
-
-    loop(1, shards, send_line)
+        remote(notes_ref, held_notes_ref.at[height], note_send, note_recv, peer, head).start()
+
+    def first_copy(quad, step):
+        there = lax.rem(head + step, HEADS)
+        return remote(
+            rows_ref.at[quad, pl.ds(pl.multiple_of(there * 64, 64), 64)],
+            spread_rows.at[head, quad],
+            first_send,
+            first_recv.at[head, quad],
+            me,
+            there,
+        )
+
+    for step in (0, 3, 2, 1):
+        quad = lax.rem(height // 4 + step, 4)
+        for way in range(1, HEADS):
+            first_copy(quad, way).start()
+        own = rows_ref.at[quad, pl.ds(pl.multiple_of(head * 64, 64), 64)]
+        pltpu.make_async_copy(own, spread_rows.at[head, quad], first_recv.at[head, quad]).start()
+
+    def stay_copy():
+        return pltpu.make_async_copy(
+            spread_rows.at[lax.rem(height, HEADS), height // 4], full.at[height, head], stay_sem
+        )
+
+    def send_quarters(turn):
+        there = lax.rem(height // 2 - OUTWARD[turn] + 8, 8)
+
+        def send_quarter(side):
+            plane = there * 2 + side
+            row_head, quad = (lax.rem(plane, HEADS), plane // 4)
+            source = spread_rows.at[row_head, quad]
+            pltpu.make_async_copy(source, source, first_recv.at[row_head, quad]).wait()
+
+            @pl.when(plane == height)
+            def _():
+                stay_copy().start()
+
+            @pl.when(plane != height)
+            def _():
+                remote(
+                    source, full.at[height, head], z_send, z_recv.at[height],
+                    device_at(column, plane, core), head,
+                ).start()
+
+        loop(0, 2, send_quarter)
+
+    for turn in range(AHEAD):
+        send_quarters(turn)
+    loop(1, RING, send_notes)
 
     def y_copy(source, quarter, step, kind):
         part = full.at[source, around(quarter, HEADS)]
@@ -139,13 +160,21 @@
         )
 
     def pair_at(turn):
-        return lax.rem(height // 2 + NEAR_FIRST[turn] + 8, 8)
+        return lax.rem(height // 2 + OUTWARD[turn] + 8, 8)
 
     def share(turn):
         for side in range(2):
             source = pair_at(turn) * 2 + side
             part = full.at[source, head]
-            remote(part, part, z_send, z_recv.at[source], me, head).wait_recv()
+
+            @pl.when(source == height)
+            def _():
+                stay_copy().wait()
+
+            @pl.when(source != height)
+            def _():
+                remote(part, part, z_send, z_recv.at[source], me, other).wait_recv()
+
             y_copy(source, head, 1, 0).start()
             y_copy(source, head, -1, 1).start()
 
@@ -165,10 +194,10 @@
         pair = pair_at(turn)
         for side in range(2):
             y_copy(pair * 2 + side, head + 2, 1, 2).wait_recv()
-        table = hit_table(held_slots_ref[pair * 2], held_slots_ref[pair * 2 + 1], head)
+        table = hit_table(held_notes_ref, pair, head)
         tokens = full[pl.ds(pair * 2, 2)].reshape(512, 512)
         result = jnp.dot(table, tokens, preferred_element_type=jnp.float32)
-        packed[turn] = result.astype(jnp.bfloat16).reshape(PEERS, 64, 512)
+        packed[turn] = result.astype(jnp.bfloat16).reshape(PEERS, 4, 16, 512)
         target = boxes_ref.at[mine * 8 + pair]
         pltpu.make_async_copy(packed.at[turn, mine], target, own_sem.at[turn]).start()
 
@@ -181,15 +210,28 @@
 
         loop(1, PEERS, send)
 
-    other = lax.rem(head + 1, HEADS)
+    def send_lines(step):
+        peer = lax.rem(mine + step, PEERS)
+        remote(
+            held_notes_ref.at[pl.ds(0, RING), 4 + peer], lines_ref.at[mine], line_send, line_recv,
+            device_at(peer // 2, height, lax.rem(peer, 2)), head,
+        ).start()
+
+    own_lines = pltpu.make_async_copy(
+        held_notes_ref.at[pl.ds(0, RING), 4 + mine], lines_ref.at[mine], line_own
+    )
     for turn in range(10):
         if turn < 8:
             share(turn)
+        if turn + AHEAD < 8:
+            send_quarters(turn + AHEAD)
         if 1 <= turn < 9:
             relay(turn - 1)
         if turn == 2:
-            lot = held_slots_ref.at[pl.ds(0, RING - 1)]
-            remote(lot, lot, slot_send, slot_recv, me, other).wait()
+            lot = held_notes_ref.at[pl.ds(0, RING - 1)]
+            remote(lot, lot, note_send, note_recv, me, other).wait()
+            own_lines.start()
+            loop(1, PEERS, send_lines)
         if turn >= 2:
             deliver(turn - 2)
     for turn in range(8):
@@ -198,7 +240,8 @@
         ).wait()
     lot = boxes_ref.at[pl.ds(0, 56)]
     remote(lot, lot, x_send, x_recv, me, other).wait()
-    lot = held_lines_ref.at[pl.ds(0, shards - 1)]
+    own_lines.wait()
+    lot = lines_ref.at[pl.ds(0, PEERS - 1)]
     remote(lot, lot, line_send, line_recv, me, other).wait()
     lot = full.at[pl.ds(0, 12)]
     remote(lot, lot, y_send, y_recv.at[0, 0], me, other).wait_send()
@@ -207,35 +250,102 @@
         part = full.at[0, 0]
         remote(part, part, z_send, z_recv.at[0], me, other).wait_send()
 
-    loop(0, RING - jnp.where(here, 1, 0), sent_quarter)
-
-
-def spread(rows, slots, lines, shards):
+    loop(0, RING - 1, sent_quarter)
+    lot = spread_rows.at[pl.ds(0, HEADS - 1)]
+    remote(lot, lot, first_send, first_recv.at[0, 0], me, other).wait_send()
+
+
+def spread(rows, notes):
     vmem = pl.BlockSpec(memory_space=pltpu.VMEM)
     dma = pltpu.SemaphoreType.DMA
     return pl.pallas_call(
-        functools.partial(spread_kernel, shards),
+        spread_kernel,
         out_shape=(
-            jax.ShapeDtypeStruct((64, 64, 512), jnp.bfloat16),
-            jax.ShapeDtypeStruct((RING,) + slots.shape, jnp.int32),
-            jax.ShapeDtypeStruct((shards,) + lines.shape[1:], jnp.int32),
+            jax.ShapeDtypeStruct((64, 4, 16, 512), jnp.bfloat16),
+            jax.ShapeDtypeStruct((RING,) + notes.shape, jnp.int32),
+            jax.ShapeDtypeStruct((PEERS, RING) + notes.shape[1:], jnp.int32),
         ),
-        in_specs=[vmem] * 3,
+        in_specs=[vmem] * 2,
         out_specs=(vmem,) * 3,
         scratch_shapes=[
+            pltpu.VMEM((HEADS, 4, 64, 512), jnp.bfloat16),
             pltpu.VMEM((RING, 4, 64, 512), jnp.bfloat16),
-            pltpu.VMEM((8, PEERS, 64, 512), jnp.bfloat16),
-            dma, dma, dma, dma,
+            pltpu.VMEM((8, PEERS, 4, 16, 512), jnp.bfloat16),
+            dma, dma, dma, dma, dma,
+            dma, dma((HEADS, 4)), dma,
             dma, dma((RING,)), dma, dma((3, RING)), dma, dma, dma((8,)),
         ],
         compiler_params=pltpu.CompilerParams(
             collective_id=0, has_side_effects=True, vmem_limit_bytes=48 * 2**20
         ),
-    )(rows, slots, lines)
+    )(rows, notes)
+
+
+def product(left, right, left_dim, right_dim):
+    return lax.dot_general(
+        left, right, (((left_dim,), (right_dim,)), ((), ())), preferred_element_type=jnp.float32
+    )
+
+
+def attend_kernel(lines_ref, rows_ref, boxes_ref, sums_ref, results):
+    scale = 1.0 / math.sqrt(HEAD_DIM)
+    shape = (512, 1024)
+    row = lax.broadcasted_iota(jnp.int32, shape, 0)
+    table = jnp.where(lines_ref[0] == row, 1.0, 0.0).astype(jnp.bfloat16)
+    grouped = product(table, rows_ref[...].reshape(1024, 512), 1, 0).astype(jnp.bfloat16)
+    size = (CLUSTER_SIZE, CLUSTER_SIZE)
+    allowed = lax.broadcasted_iota(jnp.int32, size, 1) <= lax.broadcasted_iota(jnp.int32, size, 0)
+    sums_ref[...] = jnp.zeros_like(sums_ref)
+    for cluster in range(2):
+        first = cluster * CLUSTER_SIZE
+        query, key, value, grad = (
+            grouped[first : first + CLUSTER_SIZE, i * HEAD_DIM : (i + 1) * HEAD_DIM]
+            for i in range(4)
+        )
+        scores = jnp.where(allowed, product(query, key, 1, 1) * scale, jnp.float32(-1e30))
+        weights = jnp.exp(scores - jnp.max(scores, axis=1, keepdims=True))
+        attention = weights / jnp.sum(weights, axis=1, keepdims=True)
+        attn_low = attention.astype(jnp.bfloat16)
+        prob_grad = product(grad, value, 1, 1)
+        row_dot = jnp.sum(attention * prob_grad, axis=1, keepdims=True)
+        grad_score = (attention * (prob_grad - row_dot) * scale).astype(jnp.bfloat16)
+        outs = (
+            product(attn_low, value, 1, 0),
+            product(grad_score, key, 1, 0),
+            product(grad_score, query, 0, 0),
+            product(attn_low, grad, 0, 0),
+        )
+        for i, out in enumerate(outs):
+            results[first : first + CLUSTER_SIZE, i * HEAD_DIM : (i + 1) * HEAD_DIM] = out.astype(
+                jnp.bfloat16
+            )
+        key_float = key.astype(jnp.float32)
+        normed = key_float * lax.rsqrt(
+            jnp.mean(key_float * key_float, axis=1, keepdims=True) + 1e-06
+        )
+        sums_ref[0, cluster : cluster + 1] = jnp.sum(normed, axis=0, keepdims=True)
+    boxes = product(table, results[...], 0, 0)
+    boxes_ref[...] = boxes.astype(jnp.bfloat16).reshape(64, 1, 16, 512)
+
+
+def attend_groups(lines, boxes):
+    box_spec = pl.BlockSpec((64, 1, 16, 512), lambda group: (0, group, 0, 0))
+    return pl.pallas_call(
+        attend_kernel,
+        grid=(4,),
+        out_shape=(
+            jax.ShapeDtypeStruct(boxes.shape, jnp.bfloat16),
+            jax.ShapeDtypeStruct((4, 8, HEAD_DIM), jnp.float32),
+        ),
+        in_specs=[pl.BlockSpec((1, 1, 1024), lambda group: (group, 0, 0)), box_spec],
+        out_specs=(box_spec, pl.BlockSpec((1, 8, HEAD_DIM), lambda group: (group, 0, 0))),
+        scratch_shapes=[pltpu.VMEM((512, 512), jnp.bfloat16)],
+        compiler_params=pltpu.CompilerParams(vmem_limit_bytes=48 * 2**20),
+    )(lines, boxes)
 
 
 def collect_kernel(
-    boxes_ref, held_slots_ref, sums_ref, rows_ref, means_ref,
+    boxes_ref, held_notes_ref, sums_ref, rows_ref, means_ref,
     held, part, far, near, done, sums, x_send, x_recv, own_sem,
     y_send, far_recv, near_recv, z_send, z_recv, sum_send, sum_recv,
 ):
@@ -274,9 +384,9 @@
     )
 
     def pair_at(turn):
-        return lax.rem(height // 2 + FAR_FIRST[turn] + 8, 8)
-
-    for turn in range(8):
+        return lax.rem(height // 2 + RETURN[turn] + 8, 8)
+
+    def send_boxes(turn):
         pair = pair_at(turn)
         pltpu.make_async_copy(
             boxes_ref.at[mine * 8 + pair], held.at[pair, mine], own_sem.at[turn]
@@ -290,6 +400,9 @@
             ).start()
 
         loop(1, PEERS, send_box)
+
+    for turn in range(AHEAD):
+        send_boxes(turn)
 
     def send_sum(index):
         group = index // 4
@@ -328,7 +441,7 @@
         ).wait()
         lot = held.at[pair, pl.ds(0, PEERS - 1)]
         remote(lot, lot, x_send, x_recv.at[pair], me, around(head + 1, HEADS)).wait_recv()
-        table = hit_table(held_slots_ref[pair * 2], held_slots_ref[pair * 2 + 1], head)
+        table = hit_table(held_notes_ref, pair, head)
         result = lax.dot_general(
             table, held[pair].reshape(512, 512), (((0,), (0,)), ((), ())),
             preferred_element_type=jnp.float32,
@@ -377,6 +490,8 @@
     for turn in range(10):
         if turn < 8:
             unpack(turn)
+        if turn + AHEAD < 8:
+            send_boxes(turn + AHEAD)
         if 1 <= turn < 9:
             join(turn - 1)
         if turn >= 2:
@@ -404,7 +519,7 @@
     remote(rows_ref, rows_ref, z_send, z_recv, me, other).wait_recv()
 
 
-def collect(boxes, held_slots, sums):
+def collect(boxes, held_notes, sums):
     vmem = pl.BlockSpec(memory_space=pltpu.VMEM)
     dma = pltpu.SemaphoreType.DMA
     return pl.pallas_call(
@@ -416,7 +531,7 @@
         in_specs=[vmem] * 3,
         out_specs=(vmem,) * 2,
         scratch_shapes=[
-            pltpu.VMEM((8, PEERS, 64, 512), jnp.bfloat16),
+            pltpu.VMEM((8, PEERS, 4, 16, 512), jnp.bfloat16),
             pltpu.VMEM((RING, 4, 64, 512), jnp.bfloat16),
             pltpu.VMEM((RING, 64, 512), jnp.bfloat16),
             pltpu.VMEM((2, RING, 64, 512), jnp.bfloat16),
@@ -428,59 +543,12 @@
         compiler_params=pltpu.CompilerParams(
             collective_id=1, has_side_effects=True, vmem_limit_bytes=48 * 2**20
         ),
-    )(boxes, held_slots, sums)
-
-
-def attend(query_rows, key_rows, value_rows, score_scale):
-    scores = (
-        jnp.einsum("cqhd,ckhd->chqk", query_rows, key_rows, preferred_element_type=jnp.float32)
-        * score_scale
-    )
-    slot_order = jnp.arange(query_rows.shape[1], dtype=jnp.int32)
-    allowed = slot_order[None, :] <= slot_order[:, None]
-    scores = jnp.where(allowed, scores, jnp.float32(-1e30))
-    row_max = jnp.max(scores, axis=3, keepdims=True)
-    weights = jnp.exp(scores - row_max)
-    attention = weights / jnp.sum(weights, axis=3, keepdims=True)
-    attn_low = attention.astype(jnp.bfloat16)
-    attended = jnp.einsum(
-        "chqk,ckhd->cqhd", attn_low, value_rows, preferred_element_type=jnp.float32
-    )
-    return (attention, attn_low, attended.astype(jnp.bfloat16))
-
-
-def backprop(query_rows, key_rows, value_rows, grad_rows, attention, attn_low, score_scale):
-    prob_grad = jnp.einsum(
-        "cqhd,ckhd->chqk", grad_rows, value_rows, preferred_element_type=jnp.float32
-    )
-    row_dot = jnp.sum(attention * prob_grad, axis=3, keepdims=True)
-    grad_score = (attention * (prob_grad - row_dot) * score_scale).astype(jnp.bfloat16)
-    grad_query = jnp.einsum(
-        "chqk,ckhd->cqhd", grad_score, key_rows, preferred_element_type=jnp.float32
-    )
-    grad_key = jnp.einsum(
-        "chqk,cqhd->ckhd", grad_score, query_rows, preferred_element_type=jnp.float32
-    )
-    grad_value = jnp.einsum(
-        "chqk,cqhd->ckhd", attn_low, grad_rows, preferred_element_type=jnp.float32
-    )
-    return (
-        grad_query.astype(jnp.bfloat16),
-        grad_key.astype(jnp.bfloat16),
-        grad_value.astype(jnp.bfloat16),
-    )
-
-
-def key_centroids(key_rows):
-    key_float = key_rows.astype(jnp.float32)
-    normed = key_float * lax.rsqrt(jnp.mean(key_float * key_float, axis=3, keepdims=True) + 1e-06)
-    return jnp.sum(normed, axis=(1, 2))
+    )(boxes, held_notes, sums)
 
 
 def local(queries, keys, values, out_grad, cluster_ids, slots):
     tok_rows = queries.shape[0]
     shards = lax.axis_size("seq")
-    score_scale = 1.0 / math.sqrt(HEAD_DIM)
     groups = (cluster_ids // 2).reshape(-1)
     group_hits = (groups[:, None] == jnp.arange(shards, dtype=jnp.int32)[None, :]).astype(jnp.int32)
     earlier = jnp.cumsum(group_hits, axis=0) - group_hits
@@ -490,42 +558,23 @@
     lines = lax.dynamic_index_in_dim(
         routing.reshape(4, HEADS, 2, 32), lax.axis_index("head"), axis=1, keepdims=False
     )
-    lines = jnp.pad(lines.reshape(PEERS, 1, 32), ((0, 0), (0, 0), (0, 96)))
-    slot_row = buffer_slot.reshape(tok_rows, 2).T.reshape(1, 2 * tok_rows)
+    lines = jnp.pad(lines.reshape(PEERS, 32), ((0, 0), (0, 96)))
+    slot_rows = buffer_slot.reshape(tok_rows, 2).T.reshape(4, 128)
+    notes = jnp.concatenate([slot_rows, lines], axis=0)[:, None, :]
 
     def by_head(rows_in):
         return rows_in.reshape(tok_rows, HEADS, HEAD_DIM).transpose(1, 0, 2)
 
     sent = jnp.concatenate([by_head(a) for a in (queries, keys, values, out_grad)], axis=2)
-    arrived, held_slots, held_lines = spread(sent, slot_row, lines, shards)
-    routing_in = (
-        held_lines[:, 0, :32]
-        .reshape(4, 8, 2, 2, 4, 8)
-        .transpose(4, 0, 3, 1, 2, 5)
-        .reshape(4, 1024)
-    )
-    gather_table = (
-        routing_in[:, None, :] == jnp.arange(512, dtype=jnp.int32)[None, :, None]
-    ).astype(jnp.bfloat16)
-    arrived = arrived.reshape(64, 4, 16, 512).transpose(1, 0, 2, 3).reshape(4, 1024, 512)
-    grouped = jnp.einsum(
-        "grs,gsd->grd", gather_table, arrived, preferred_element_type=jnp.float32
-    ).astype(jnp.bfloat16)
-    query_rows, key_rows, value_rows, grad_rows = (
-        grouped[:, :, i * HEAD_DIM : (i + 1) * HEAD_DIM].reshape(8, CLUSTER_SIZE, 1, HEAD_DIM)
-        for i in range(4)
-    )
-    attention, attn_low, attended = attend(query_rows, key_rows, value_rows, score_scale)
-    sums = jnp.pad(key_centroids(key_rows).reshape(4, 2, HEAD_DIM), ((0, 0), (0, 6), (0, 0)))
-    grads = backprop(
-        query_rows, key_rows, value_rows, grad_rows, attention, attn_low, score_scale
-    )
-    results = jnp.concatenate([a.reshape(4, 512, HEAD_DIM) for a in (attended,) + grads], axis=2)
-    boxes = jnp.einsum(
-        "grs,grd->gsd", gather_table, results, preferred_element_type=jnp.float32
-    ).astype(jnp.bfloat16)
-    boxes = boxes.reshape(4, 64, 16, 512).transpose(1, 0, 2, 3).reshape(64, 64, 512)
-    rows_back, means = collect(boxes, held_slots, sums)
+    arrived, held_notes, held_lines = spread(sent, notes)
+    lines_in = (
+        held_lines[:, :, 0, :32]
+        .reshape(PEERS, RING // 2, 2, 4, 8)
+        .transpose(3, 0, 1, 2, 4)
+        .reshape(4, 1, 1024)
+    )
+    boxes, sums = attend_groups(lines_in, arrived)
+    rows_back, means = collect(boxes, held_notes, sums)
     back = rows_back.reshape(HEADS, tok_rows, 4, HEAD_DIM)
     outs = tuple(
         back[:, :, i].transpose(1, 0, 2).reshape(tok_rows, HEADS * HEAD_DIM) for i in range(4)

time: 268 us -> 220 us (0.82)
  matrix products: 23.9 us -> 0 us
  Pallas kernels: 212 us -> 198 us
  local copies, waits for them, and re-layouts: 22.5 us -> 16.6 us
    dot_general x7 -> x0, matrix products: 20.6 us -> none  [the longest x1 4.91 us: local(): jnp.einsum('grs,gsd->grd', gather_table, arrived, preferred_element_type=...]
    pallas_call x1 -> x2, Pallas kernels: 132 us -> 118 us  [the longest x1 106 us: spread(): pl.pallas_call(spread_kernel, out_shape=(jax.ShapeDtypeStruct((64, 4, 16,...]
    convert_element_type x4 -> x0, local copies, waits for them, and re-layouts: 4.74 us -> none  [the longest x1 1.4 us: backprop(): grad_key.astype(jnp.bfloat16)]
    sub x1 -> x0, matrix products: 3.35 us -> none  [attend(): weights = jnp.exp(scores - row_max)]
    unnamed x26 -> x21, local copies, waits for them, and re-layouts: 5.59 us -> 7.48 us
where the time goes in v4:
time: 220 us; the launch traced here: 217 us
  Pallas kernels  198 us (90%)
  local copies, waits for them, and re-layouts  16.6 us (8%)
    pallas_call x1, Pallas kernels, spread(): pl.pallas_call(spread_kernel, out_shape=(jax.ShapeDtypeStruct((64, 4, 16,...  106 us
    pallas_call x1, Pallas kernels, collect(): pl.pallas_call(collect_kernel, out_shape=(jax.ShapeDtypeStruct((4, 4, 64,...  80.8 us
    pallas_call x1, Pallas kernels, attend_groups(): pl.pallas_call(attend_kernel, grid=(4,), out_shape=(jax.ShapeDtypeStruct(...  11.5 us
    unnamed x21, local copies, waits for them, and re-layouts  7.48 us

profile of v4, /device:TPU:1, one launch (start us, length us, event | category | flops | bytes accessed | tf_op | source)
XLA Modules:
  0.0 217.4 jit_solution(6172943665923815295)
XLA Ops:
  0.6 0.7 broadcast_compare_fusion
  1.4 0.2 copy.53
  1.6 0.8 copy.58
  2.4 0.8 copy.48
  3.5 0.1 reshape.120
  3.6 0.1 eq.31
  3.8 0.1 eq.27
  4.0 0.2 fusion.2
  4.4 0.2 fusion.1
  4.6 2.6 %scatter_custom_fusion = s32[1024]{0:T(1024)S(1)} fusion(s32[512]{0:T(512)S(1)} %bitcast.74, s32[512]{0:T(512)S(1)} %reshape.120, s32[]{:T(128)} %constant.41.clone.1), kind=kCustom, calls=%fused_computation.28 | custom fusion | bytes 4100 | tf_op jit(solution)/shard_map/scatter | solution.py:557
  7.8 0.2 copy.41
  8.1 0.2 copy.43
  8.5 0.2 copy.45
  8.8 0.2 copy.47
  9.1 106.0 %shard_map.101 = (bf16[64,4,16,512]{3,2,1,0:T(8,128)(2,1)S(1)}, s32[16,12,1,128]{3,2,1,0:T(1,128)S(1)}, s32[8,16,1,128]{3,2,1,0:T(1,128)S(1)}) custom-call(bf16[4,256,512]{2,1,0:T(8,128)(2,1)S(1)} %pad_maximum_fusion.rows_ref, s32[12,1,128]{2,1,0:T(1,128)S(1)} %broadcast_in_dim.9.notes_ref), custom_call_target="tpu_custom_call" | custom-call | tf_op jit(solution)/shard_map/pallas_call | solution.py:261
  115.1 1.9 copy-done
  117.0 0.2 slice_reduce_fusion
  117.2 0.2 reshape_squeeze.3
  117.5 0.4 reshape.110.lines_ref
  117.9 11.5 %shard_map.102 = (bf16[64,4,16,512]{3,2,1,0:T(8,128)(2,1)S(1)}, f32[4,8,128]{2,1,0:T(8,128)S(1)}) custom-call(s32[4,1,1024]{2,1,0:T(1,128)S(1)} %reshape.110.lines_ref, bf16[64,4,16,512]{3,2,1,0:T(8,128)(2,1)} %copy-done), custom_call_target="tpu_custom_call" | custom-call | tf_op jit(solution)/shard_map/pallas_call | solution.py:333
  129.4 80.8 %shard_map.103 = (bf16[4,4,64,512]{3,2,1,0:T(8,128)(2,1)S(1)}, f32[8,128]{1,0:T(8,128)S(1)}) custom-call(bf16[64,4,16,512]{3,2,1,0:T(8,128)(2,1)S(1)} %get-tuple-element.14.boxes_ref, s32[16,12,1,128]{3,2,1,0:T(1,128)S(1)} %get-tuple-element.15.held_notes_ref, f32[4,8,128]{2,1,0:T(8,128)S(1)} %get-tuple-element.16.sums_ref), custom_call_target="tpu_custom_call" | custom-call | tf_op jit(solution)/shard_map/pallas_call | solution.py:525
  210.2 0.3 reshape.111
  210.5 0.6 slice.31
  211.1 1.5 fusion.11
  212.6 0.4 copy.85
  213.0 0.8 copy.71
  213.8 0.3 copy.84
  214.2 0.8 copy.70
  215.0 0.3 copy.83
  215.4 0.8 copy.69
  216.2 0.3 copy.82
  216.6 0.8 copy.68
  (33 shorter events, 1.7 us)
Async XLA Ops:
  0.6 7.0 %copy-start.1 = (bf16[256,512]{1,0:T(8,128)(2,1)S(1)}, bf16[256,512]{1,0:T(8,128)(2,1)}, u32[]{:S(2)}) copy-start(bf16[256,512]{1,0:T(8,128)(2,1)} %param.6) | copy-start | bytes 786436
  3.3 4.6 %copy-start.2 = (bf16[256,512]{1,0:T(8,128)(2,1)S(1)}, bf16[256,512]{1,0:T(8,128)(2,1)}, u32[]{:S(2)}) copy-start(bf16[256,512]{1,0:T(8,128)(2,1)} %param.7) | copy-start | bytes 786436
  4.2 4.1 %copy-start.3 = (bf16[256,512]{1,0:T(8,128)(2,1)S(1)}, bf16[256,512]{1,0:T(8,128)(2,1)}, u32[]{:S(2)}) copy-start(bf16[256,512]{1,0:T(8,128)(2,1)} %param.8) | copy-start | bytes 786436
  4.4 4.3 %copy-start.4 = (bf16[256,512]{1,0:T(8,128)(2,1)S(1)}, bf16[256,512]{1,0:T(8,128)(2,1)}, u32[]{:S(2)}) copy-start(bf16[256,512]{1,0:T(8,128)(2,1)} %param.9) | copy-start | bytes 786436
  115.1 1.9 copy-start

commit v5 on v4

--- a/solution.py
+++ b/solution.py
@@ -14,9 +14,10 @@
 HEADS = 4
 PEERS = 8
 MESH = pl.DeviceIdType.MESH
-OUTWARD = (0, 1, 4, -3, -2, 3, 2, -1)
+OUTWARD = (0, 1, -2, -1, 2, 3, 4, -3)
 RETURN = (4, 3, -2, -3, 2, 1, 0, -1)
 AHEAD = 3
+BACK_AHEAD = 8
 
 
 def place():
@@ -401,7 +402,7 @@
 
         loop(1, PEERS, send_box)
 
-    for turn in range(AHEAD):
+    for turn in range(BACK_AHEAD):
         send_boxes(turn)
 
     def send_sum(index):
@@ -490,8 +491,8 @@
     for turn in range(10):
         if turn < 8:
             unpack(turn)
-        if turn + AHEAD < 8:
-            send_boxes(turn + AHEAD)
+        if turn + BACK_AHEAD < 8:
+            send_boxes(turn + BACK_AHEAD)
         if 1 <= turn < 9:
             join(turn - 1)
         if turn >= 2:
@@ -546,26 +547,80 @@
     )(boxes, held_notes, sums)
 
 
+def prepare_kernel(
+    queries_ref, keys_ref, values_ref, grads_ref, ids_ref, slots_ref, rows_ref, notes_ref
+):
+    head = lax.axis_index("head")
+    for i, source in enumerate((queries_ref, keys_ref, values_ref, grads_ref)):
+        for quad in range(HEADS):
+            rows_ref[quad, :, i * HEAD_DIM : (i + 1) * HEAD_DIM] = source[
+                :, quad * HEAD_DIM : (quad + 1) * HEAD_DIM
+            ]
+    count = ids_ref.shape[0]
+    copies = 2 * count
+
+    def iota(shape, dim):
+        return lax.broadcasted_iota(jnp.int32, shape, dim)
+
+    def ones_where(condition):
+        return jnp.where(condition, 1.0, 0.0).astype(jnp.bfloat16)
+
+    square = (count, count)
+    unit = ones_where(iota(square, 0) == iota(square, 1))
+
+    def as_row(column_ref):
+        turned = product(column_ref[...].astype(jnp.float32).astype(jnp.bfloat16), unit, 0, 0)
+        return jnp.concatenate([turned[0:1], turned[1:2]], axis=1)
+
+    ids = as_row(ids_ref).astype(jnp.int32)
+    slots = as_row(slots_ref)
+    groups = ids // 2
+    hit = iota((128, copies), 0) == groups
+    before = ones_where(iota((copies, copies), 0) < iota((copies, copies), 1))
+    earlier = product(ones_where(hit), before, 1, 0)
+    rank = jnp.sum(jnp.where(hit, earlier, 0.0), axis=0, keepdims=True)
+    spots = groups * 8 + rank.astype(jnp.int32)
+    shape = (PEERS * 128, copies)
+    row = iota(shape, 0)
+    peer, line = (row // 128, row % 128)
+    device = ((peer // 2) * HEADS + head) * 2 + peer % 2
+    wanted = jnp.where(line < 32, device * 32 + line, -1)
+    kind = iota((8, copies), 0)
+    local_ids = (ids % 2).astype(jnp.float32)
+    facts = jnp.where(
+        kind == 0, slots, jnp.where(kind == 1, local_ids, jnp.where(kind == 2, 1.0, 0.0))
+    ).astype(jnp.bfloat16)
+    found = product(facts, ones_where(spots == wanted), 1, 1)
+    lines = (found[0:1] + CLUSTER_SIZE * found[1:2] + found[2:3] - 1.0).astype(jnp.int32)
+    for part in range(4):
+        notes_ref[part] = spots[:, part * 128 : (part + 1) * 128]
+    for part in range(PEERS):
+        notes_ref[4 + part] = lines[:, part * 128 : (part + 1) * 128]
+
+
+def finish_kernel(rows_ref, means_in_ref, out_ref, query_ref, key_ref, value_ref, means_ref):
+    for quad in range(HEADS):
+        rows = rows_ref[quad].reshape(256, 512)
+        for i, target in enumerate((out_ref, query_ref, key_ref, value_ref)):
+            target[:, quad * HEAD_DIM : (quad + 1) * HEAD_DIM] = rows[
+                :, i * HEAD_DIM : (i + 1) * HEAD_DIM
+            ]
+    means_ref[...] = means_in_ref[0:2]
+
+
 def local(queries, keys, values, out_grad, cluster_ids, slots):
-    tok_rows = queries.shape[0]
-    shards = lax.axis_size("seq")
-    groups = (cluster_ids // 2).reshape(-1)
-    group_hits = (groups[:, None] == jnp.arange(shards, dtype=jnp.int32)[None, :]).astype(jnp.int32)
-    earlier = jnp.cumsum(group_hits, axis=0) - group_hits
-    buffer_slot = groups * 8 + jnp.sum(earlier * group_hits, axis=1)
-    targets = (cluster_ids % 2 * CLUSTER_SIZE + slots).reshape(-1)
-    routing = jnp.full((shards * 8,), -1, jnp.int32).at[buffer_slot].set(targets)
-    lines = lax.dynamic_index_in_dim(
-        routing.reshape(4, HEADS, 2, 32), lax.axis_index("head"), axis=1, keepdims=False
-    )
-    lines = jnp.pad(lines.reshape(PEERS, 32), ((0, 0), (0, 96)))
-    slot_rows = buffer_slot.reshape(tok_rows, 2).T.reshape(4, 128)
-    notes = jnp.concatenate([slot_rows, lines], axis=0)[:, None, :]
-
-    def by_head(rows_in):
-        return rows_in.reshape(tok_rows, HEADS, HEAD_DIM).transpose(1, 0, 2)
-
-    sent = jnp.concatenate([by_head(a) for a in (queries, keys, values, out_grad)], axis=2)
+    vmem = pl.BlockSpec(memory_space=pltpu.VMEM)
+    params = pltpu.CompilerParams(vmem_limit_bytes=32 * 2**20)
+    sent, notes = pl.pallas_call(
+        prepare_kernel,
+        out_shape=(
+            jax.ShapeDtypeStruct((HEADS, 256, 512), jnp.bfloat16),
+            jax.ShapeDtypeStruct((4 + PEERS, 1, 128), jnp.int32),
+        ),
+        in_specs=[vmem] * 6,
+        out_specs=(vmem,) * 2,
+        compiler_params=params,
+    )(queries, keys, values, out_grad, cluster_ids, slots)
     arrived, held_notes, held_lines = spread(sent, notes)
     lines_in = (
         held_lines[:, :, 0, :32]
@@ -575,11 +630,14 @@
     )
     boxes, sums = attend_groups(lines_in, arrived)
     rows_back, means = collect(boxes, held_notes, sums)
-    back = rows_back.reshape(HEADS, tok_rows, 4, HEAD_DIM)
-    outs = tuple(
-        back[:, :, i].transpose(1, 0, 2).reshape(tok_rows, HEADS * HEAD_DIM) for i in range(4)
-    )
-    return outs + (means[:2],)
+    whole = jax.ShapeDtypeStruct(queries.shape, jnp.bfloat16)
+    return pl.pallas_call(
+        finish_kernel,
+        out_shape=(whole,) * 4 + (jax.ShapeDtypeStruct((2, HEAD_DIM), jnp.float32),),
+        in_specs=[vmem] * 2,
+        out_specs=(vmem,) * 5,
+        compiler_params=params,
+    )(rows_back, means)
 
 
 def solution(mesh):

time: 220 us -> 208 us (0.945)
  the two profiles are of different devices: /device:TPU:1 before, /device:TPU:57 now
where the time goes in v5:
time: 208 us; the launch traced here: 207 us
  Pallas kernels  198 us (95%)
  local copies, waits for them, and re-layouts  8.2 us (4%)
    pallas_call x1, Pallas kernels, spread(): pl.pallas_call(spread_kernel, out_shape=(jax.ShapeDtypeStruct((64, 4, 16,...  102 us
    pallas_call x1, Pallas kernels, collect(): pl.pallas_call(collect_kernel, out_shape=(jax.ShapeDtypeStruct((4, 4, 64,...  82.8 us
    pallas_call x1, Pallas kernels, attend_groups(): pl.pallas_call(attend_kernel, grid=(4,), out_shape=(jax.ShapeDtypeStruct(...  11.5 us
    unnamed x12, local copies, waits for them, and re-layouts  7.36 us

profile of v5, /device:TPU:57, one launch (start us, length us, event | category | flops | bytes accessed | tf_op | source)
XLA Modules:
  0.0 207.4 jit_solution(18201525716629548870)
XLA Ops:
  0.6 0.8 copy.11.ids_ref
  1.4 0.8 copy.12.slots_ref
  2.3 0.0 copy-start.1
  2.3 0.9 copy-done.1
  3.2 0.0 copy-start.2
  3.2 0.9 copy-done.2
  4.2 0.0 copy-start.3
  4.2 0.9 copy-done.3
  5.1 0.0 copy-start.4
  5.1 0.9 copy-done.4
  6.1 1.0 shard_map.101
  7.0 102.0 %shard_map.102 = (bf16[64,4,16,512]{3,2,1,0:T(8,128)(2,1)S(1)}, s32[16,12,1,128]{3,2,1,0:T(1,128)S(1)}, s32[8,16,1,128]{3,2,1,0:T(1,128)S(1)}) custom-call(bf16[4,256,512]{2,1,0:T(8,128)(2,1)S(1)} %get-tuple-element.14.rows_ref, s32[12,1,128]{2,1,0:T(1,128)S(1)} %get-tuple-element.15.notes_ref), custom_call_target="tpu_custom_call" | custom-call | tf_op jit(solution)/shard_map/pallas_call | solution.py:262
  109.1 0.0 copy-start
  109.1 1.9 copy-done
  111.0 0.2 slice_reduce_fusion
  111.2 0.2 reshape_squeeze.3
  111.3 0.1 copy.15
  111.5 0.4 reshape.13.lines_ref
  111.9 11.5 %shard_map.103 = (bf16[64,4,16,512]{3,2,1,0:T(8,128)(2,1)S(1)}, f32[4,8,128]{2,1,0:T(8,128)S(1)}) custom-call(s32[4,1,1024]{2,1,0:T(1,128)S(1)} %reshape.13.lines_ref, bf16[64,4,16,512]{3,2,1,0:T(8,128)(2,1)} %copy-done), custom_call_target="tpu_custom_call" | custom-call | tf_op jit(solution)/shard_map/pallas_call | solution.py:334
  123.4 82.8 %shard_map.104 = (bf16[4,4,64,512]{3,2,1,0:T(8,128)(2,1)S(1)}, f32[8,128]{1,0:T(8,128)S(1)}) custom-call(bf16[64,4,16,512]{3,2,1,0:T(8,128)(2,1)S(1)} %get-tuple-element.18.boxes_ref, s32[16,12,1,128]{3,2,1,0:T(1,128)S(1)} %get-tuple-element.19.held_notes_ref, f32[4,8,128]{2,1,0:T(8,128)S(1)} %get-tuple-element.20.sums_ref), custom_call_target="tpu_custom_call" | custom-call | tf_op jit(solution)/shard_map/pallas_call | solution.py:526
  206.2 1.1 shard_map.105
Async XLA Ops:
  2.3 1.0 copy-start.1
  3.2 0.9 copy-start.2
  4.2 0.9 copy-start.3
  5.1 0.9 copy-start.4
  109.1 1.9 copy-start

commit v6 on v5

--- a/solution.py
+++ b/solution.py
@@ -14,7 +14,7 @@
 HEADS = 4
 PEERS = 8
 MESH = pl.DeviceIdType.MESH
-OUTWARD = (0, 1, -2, -1, 2, 3, 4, -3)
+OUTWARD = (0, 1, -1, 2, -2, 3, -3, 4)
 RETURN = (4, 3, -2, -3, 2, 1, 0, -1)
 AHEAD = 3
 BACK_AHEAD = 8
@@ -548,14 +548,20 @@
 
 
 def prepare_kernel(
-    queries_ref, keys_ref, values_ref, grads_ref, ids_ref, slots_ref, rows_ref, notes_ref
+    queries_ref, keys_ref, values_ref, grads_ref, ids_ref, slots_ref, rows_ref, notes_ref, move_sem
 ):
     head = lax.axis_index("head")
-    for i, source in enumerate((queries_ref, keys_ref, values_ref, grads_ref)):
-        for quad in range(HEADS):
-            rows_ref[quad, :, i * HEAD_DIM : (i + 1) * HEAD_DIM] = source[
-                :, quad * HEAD_DIM : (quad + 1) * HEAD_DIM
-            ]
+    moves = [
+        pltpu.make_async_copy(
+            source.at[:, pl.ds(quad * HEAD_DIM, HEAD_DIM)],
+            rows_ref.at[quad, :, pl.ds(i * HEAD_DIM, HEAD_DIM)],
+            move_sem.at[i, quad],
+        )
+        for i, source in enumerate((queries_ref, keys_ref, values_ref, grads_ref))
+        for quad in range(HEADS)
+    ]
+    for move in moves:
+        move.start()
     count = ids_ref.shape[0]
     copies = 2 * count
 
@@ -596,6 +602,8 @@
         notes_ref[part] = spots[:, part * 128 : (part + 1) * 128]
     for part in range(PEERS):
         notes_ref[4 + part] = lines[:, part * 128 : (part + 1) * 128]
+    for move in moves:
+        move.wait()
 
 
 def finish_kernel(rows_ref, means_in_ref, out_ref, query_ref, key_ref, value_ref, means_ref):
@@ -617,8 +625,9 @@
             jax.ShapeDtypeStruct((HEADS, 256, 512), jnp.bfloat16),
             jax.ShapeDtypeStruct((4 + PEERS, 1, 128), jnp.int32),
         ),
-        in_specs=[vmem] * 6,
+        in_specs=[pl.BlockSpec(memory_space=pl.ANY)] * 4 + [vmem] * 2,
         out_specs=(vmem,) * 2,
+        scratch_shapes=[pltpu.SemaphoreType.DMA((4, HEADS))],
         compiler_params=params,
     )(queries, keys, values, out_grad, cluster_ids, slots)
     arrived, held_notes, held_lines = spread(sent, notes)

time: 208 us -> 205 us (0.986)
  the two profiles are of different devices: /device:TPU:57 before, /device:TPU:1 now
where the time goes in v6:
time: 205 us; the launch traced here: 203 us
  Pallas kernels  194 us (95%)
  local copies, waits for them, and re-layouts  8.2 us (4%)
    pallas_call x1, Pallas kernels, spread(): pl.pallas_call(spread_kernel, out_shape=(jax.ShapeDtypeStruct((64, 4, 16,...  100 us
    pallas_call x1, Pallas kernels, collect(): pl.pallas_call(collect_kernel, out_shape=(jax.ShapeDtypeStruct((4, 4, 64,...  79.6 us
    pallas_call x1, Pallas kernels, attend_groups(): pl.pallas_call(attend_kernel, grid=(4,), out_shape=(jax.ShapeDtypeStruct(...  11.5 us
    unnamed x12, local copies, waits for them, and re-layouts  7.36 us

profile of v6, /device:TPU:1, one launch (start us, length us, event | category | flops | bytes accessed | tf_op | source)
XLA Modules:
  0.0 202.7 jit_solution(12286841208076785854)
XLA Ops:
  0.6 0.8 copy.11.ids_ref
  1.4 0.8 copy.12.slots_ref
  2.3 0.0 copy-start.1
  2.3 0.9 copy-done.1
  3.2 0.0 copy-start.2
  3.2 0.9 copy-done.2
  4.2 0.0 copy-start.3
  4.2 0.9 copy-done.3
  5.1 0.0 copy-start.4
  5.1 0.9 copy-done.4
  6.1 1.2 shard_map.101
  7.2 100.4 %shard_map.102 = (bf16[64,4,16,512]{3,2,1,0:T(8,128)(2,1)S(1)}, s32[16,12,1,128]{3,2,1,0:T(1,128)S(1)}, s32[8,16,1,128]{3,2,1,0:T(1,128)S(1)}) custom-call(bf16[4,256,512]{2,1,0:T(8,128)(2,1)S(1)} %get-tuple-element.14.rows_ref, s32[12,1,128]{2,1,0:T(1,128)S(1)} %get-tuple-element.15.notes_ref), custom_call_target="tpu_custom_call" | custom-call | tf_op jit(solution)/shard_map/pallas_call | solution.py:262
  107.6 0.0 copy-start
  107.6 1.9 copy-done
  109.6 0.2 slice_reduce_fusion
  109.7 0.2 reshape_squeeze.3
  109.9 0.1 copy.15
  110.1 0.4 reshape.13.lines_ref
  110.4 11.5 %shard_map.103 = (bf16[64,4,16,512]{3,2,1,0:T(8,128)(2,1)S(1)}, f32[4,8,128]{2,1,0:T(8,128)S(1)}) custom-call(s32[4,1,1024]{2,1,0:T(1,128)S(1)} %reshape.13.lines_ref, bf16[64,4,16,512]{3,2,1,0:T(8,128)(2,1)} %copy-done), custom_call_target="tpu_custom_call" | custom-call | tf_op jit(solution)/shard_map/pallas_call | solution.py:334
  122.0 79.6 %shard_map.104 = (bf16[4,4,64,512]{3,2,1,0:T(8,128)(2,1)S(1)}, f32[8,128]{1,0:T(8,128)S(1)}) custom-call(bf16[64,4,16,512]{3,2,1,0:T(8,128)(2,1)S(1)} %get-tuple-element.18.boxes_ref, s32[16,12,1,128]{3,2,1,0:T(1,128)S(1)} %get-tuple-element.19.held_notes_ref, f32[4,8,128]{2,1,0:T(8,128)S(1)} %get-tuple-element.20.sums_ref), custom_call_target="tpu_custom_call" | custom-call | tf_op jit(solution)/shard_map/pallas_call | solution.py:526
  201.6 1.1 shard_map.105
Async XLA Ops:
  2.3 1.0 copy-start.1
  3.2 0.9 copy-start.2
  4.2 0.9 copy-start.3
  5.1 0.9 copy-start.4
  107.6 1.9 copy-start

commit v7 on v6

--- a/solution.py
+++ b/solution.py
@@ -16,7 +16,7 @@
 MESH = pl.DeviceIdType.MESH
 OUTWARD = (0, 1, -1, 2, -2, 3, -3, 4)
 RETURN = (4, 3, -2, -3, 2, 1, 0, -1)
-AHEAD = 3
+AHEAD = 4
 BACK_AHEAD = 8
 
 
@@ -224,8 +224,6 @@
     for turn in range(10):
         if turn < 8:
             share(turn)
-        if turn + AHEAD < 8:
-            send_quarters(turn + AHEAD)
         if 1 <= turn < 9:
             relay(turn - 1)
         if turn == 2:
@@ -235,6 +233,8 @@
             loop(1, PEERS, send_lines)
         if turn >= 2:
             deliver(turn - 2)
+        if turn + AHEAD < 8:
+            send_quarters(turn + AHEAD)
     for turn in range(8):
         pltpu.make_async_copy(
             packed.at[turn, mine], boxes_ref.at[mine * 8 + turn], own_sem.at[turn]
@@ -628,7 +628,7 @@
         in_specs=[pl.BlockSpec(memory_space=pl.ANY)] * 4 + [vmem] * 2,
         out_specs=(vmem,) * 2,
         scratch_shapes=[pltpu.SemaphoreType.DMA((4, HEADS))],
-        compiler_params=params,
+        compiler_params=pltpu.CompilerParams(vmem_limit_bytes=60 * 2**20),
     )(queries, keys, values, out_grad, cluster_ids, slots)
     arrived, held_notes, held_lines = spread(sent, notes)
     lines_in = (

time: 205 us -> 206 us (level)
    pallas_call x1, Pallas kernels: 1.15 us -> 3.34 us  [local(): pl.pallas_call(prepare_kernel, out_shape=(jax.ShapeDtypeStruct((HEADS, 25...]
    pallas_call x1, Pallas kernels: 100 us -> 98.3 us  [spread(): pl.pallas_call(spread_kernel, out_shape=(jax.ShapeDtypeStruct((64, 4, 16,...]
    unnamed x12 -> x8, local copies, waits for them, and re-layouts: 7.36 us -> 6.79 us
where the time goes in v7:
time: 206 us; the launch traced here: 203 us
  Pallas kernels  195 us (95%)
  local copies, waits for them, and re-layouts  7.63 us (4%)
    pallas_call x1, Pallas kernels, spread(): pl.pallas_call(spread_kernel, out_shape=(jax.ShapeDtypeStruct((64, 4, 16,...  98.3 us
    pallas_call x1, Pallas kernels, collect(): pl.pallas_call(collect_kernel, out_shape=(jax.ShapeDtypeStruct((4, 4, 64,...  80.5 us
    pallas_call x1, Pallas kernels, attend_groups(): pl.pallas_call(attend_kernel, grid=(4,), out_shape=(jax.ShapeDtypeStruct(...  11.5 us
    unnamed x8, local copies, waits for them, and re-layouts  6.79 us

profile of v7, /device:TPU:1, one launch (start us, length us, event | category | flops | bytes accessed | tf_op | source)
XLA Modules:
  0.0 203.1 jit_solution(5034088888163167944)
XLA Ops:
  0.6 1.5 copy.11.ids_ref
  2.1 1.5 copy.12.slots_ref
  3.6 3.3 %shard_map.101 = (bf16[4,256,512]{2,1,0:T(8,128)(2,1)}, s32[12,1,128]{2,1,0:T(1,128)}) custom-call(bf16[256,512]{1,0:T(8,128)(2,1)} %queries_ref.1, bf16[256,512]{1,0:T(8,128)(2,1)} %keys_ref.1, bf16[256,512]{1,0:T(8,128)(2,1)} %values_ref.1, bf16[256,512]{1,0:T(8,128)(2,1)} %grads_ref.1, s32[256,2]{1,0:T(8,128)} %copy.11.ids_ref, s32[256,2]{1,0:T(8,128)} %copy.12.slots_ref), custom_call_target="tpu_custom_call" | custom-call | tf_op jit(solution)/shard_map/pallas_call | solution.py:622
  6.9 0.0 copy-start.1
  6.9 1.2 copy-done.1
  8.2 0.0 copy-start.2
  8.2 0.7 copy-done.2
  8.8 98.3 %shard_map.102 = (bf16[64,4,16,512]{3,2,1,0:T(8,128)(2,1)S(1)}, s32[16,12,1,128]{3,2,1,0:T(1,128)S(1)}, s32[8,16,1,128]{3,2,1,0:T(1,128)S(1)}) custom-call(bf16[4,256,512]{2,1,0:T(8,128)(2,1)S(1)} %copy-done.1, s32[12,1,128]{2,1,0:T(1,128)S(1)} %copy-done.2), custom_call_target="tpu_custom_call" | custom-call | tf_op jit(solution)/shard_map/pallas_call | solution.py:262
  107.1 0.0 copy-start
  107.1 1.9 copy-done
  109.1 0.2 slice_reduce_fusion
  109.2 0.2 reshape_squeeze.3
  109.4 0.1 copy.15
  109.6 0.4 reshape.13.lines_ref
  109.9 11.5 %shard_map.103 = (bf16[64,4,16,512]{3,2,1,0:T(8,128)(2,1)S(1)}, f32[4,8,128]{2,1,0:T(8,128)S(1)}) custom-call(s32[4,1,1024]{2,1,0:T(1,128)S(1)} %reshape.13.lines_ref, bf16[64,4,16,512]{3,2,1,0:T(8,128)(2,1)} %copy-done), custom_call_target="tpu_custom_call" | custom-call | tf_op jit(solution)/shard_map/pallas_call | solution.py:334
  121.5 80.5 %shard_map.104 = (bf16[4,4,64,512]{3,2,1,0:T(8,128)(2,1)S(1)}, f32[8,128]{1,0:T(8,128)S(1)}) custom-call(bf16[64,4,16,512]{3,2,1,0:T(8,128)(2,1)S(1)} %get-tuple-element.18.boxes_ref, s32[16,12,1,128]{3,2,1,0:T(1,128)S(1)} %get-tuple-element.19.held_notes_ref, f32[4,8,128]{2,1,0:T(8,128)S(1)} %get-tuple-element.20.sums_ref), custom_call_target="tpu_custom_call" | custom-call | tf_op jit(solution)/shard_map/pallas_call | solution.py:526
  202.0 1.1 shard_map.105
Async XLA Ops:
  6.9 1.2 copy-start.1
  8.2 0.7 copy-start.2
  107.1 1.9 copy-start
